TPU v7x, 128 devices: a whole 4x4x4 slice. The times are simulated.
128 devices in a mesh: ctx: 16 (over z, y_hi, core), exp: 8 (over y_lo, x).
Axes of the slice: x: 4, y: 4 (y_hi: 2, y_lo: 2; y = y_hi * 2 + y_lo), z: 4, core: 2. Of those that a mesh axis runs over, the one named last changes fastest.
Arguments:
- tokens: bfloat16 [2048, 2, 4096], P(('ctx', 'exp')), may hold values from -45 to 45
- queries: bfloat16 [2048, 2, 4096], P('ctx', None, 'exp'), may hold values from -7.5 to 7.5
- keys: bfloat16 [2048, 2, 256], P('ctx'), may hold values from -7.5 to 7.5
- values: bfloat16 [2048, 2, 256], P('ctx'), may hold values from -6 to 6
- output_weight: bfloat16 [4096, 4096], P('exp'), may hold values from -0.09375 to 0.09375
- norm_gain: bfloat16 [4096], replicated, may hold values from 0.25 to 1.75
- routing: int32 [2048, 2, 8], P(('ctx', 'exp')), may hold values from 0 to 127, all different within a row; in each aligned block of 32 rows (0 to 31, 32 to 63, ..., all dimensions but the last counted through in order) at most 3 rows name the same one
- gate_values: float32 [2048, 2, 8], P(('ctx', 'exp')), may hold values from 0.05 to 0.5
- expand_weight: bfloat16 [128, 4096, 1536], P(('ctx', 'exp')), may hold values from -0.09375 to 0.09375
- reduce_weight: bfloat16 [128, 768, 4096], P(('ctx', 'exp')), may hold values from -0.21875 to 0.21875
Outputs:
- layer_out: bfloat16 [2048, 2, 4096], P(('ctx', 'exp'))
Inputs may be any that keep to these rules, and one draw needn't show every extreme that they name: `routing`: in each aligned block of 32 rows (position-major, both sequences of a position together) no expert is named by more than 3 rows, a bound that some block reaches.
All inputs are finite; a program needn't handle non-finite values.
Results may differ from a plain program's by a relative error of at most 0.015.
Values may be sent and summed in bfloat16 or wider, within the bound.
No kernel may reach another device: no remote copies, remote signals or barrier semaphores. Data moves between devices by JAX's collectives and lax.ppermute only.
A program may use at most 128 MiB of HBM per device.

v0:
```python
import jax
import jax.numpy as jnp
from jax import lax
from jax.sharding import PartitionSpec as P

D = 4096
HEADS = 32
KV_HEADS = 2
HEAD_DIM = 128
EW = 768
TOP = 8


def shards(
    tokens,
    queries,
    keys,
    values,
    output_weight,
    norm_gain,
    routing,
    gate_values,
    expand_weight,
    reduce_weight,
):
    length_here = queries.shape[0]
    pair_count = queries.shape[1]
    local_heads = queries.shape[2] // HEAD_DIM
    context_size = lax.axis_size("ctx")
    expert_size = lax.axis_size("exp")
    head_group = HEADS // KV_HEADS
    key_head = lax.axis_index("exp") * local_heads // head_group
    first_query = lax.axis_index("ctx") * length_here
    query_pos = first_query + jnp.arange(length_here, dtype=jnp.int32)
    query_block = queries.reshape(length_here, pair_count, local_heads, HEAD_DIM)
    score_scale = HEAD_DIM ** (-0.5)
    start_state = (
        jnp.full((pair_count, local_heads, length_here), -1e30, jnp.float32),
        jnp.zeros((pair_count, local_heads, length_here), jnp.float32),
        jnp.zeros((pair_count, local_heads, length_here, HEAD_DIM), jnp.float32),
    )
    key_piece = lax.dynamic_slice_in_dim(
        lax.all_gather(keys, "ctx", axis=0, tiled=True), key_head * HEAD_DIM, HEAD_DIM, 2
    )
    value_piece = lax.dynamic_slice_in_dim(
        lax.all_gather(values, "ctx", axis=0, tiled=True), key_head * HEAD_DIM, HEAD_DIM, 2
    )

    def compute(state_in):
        running_max, running_sum, running_acc = state_in
        scores = (
            jnp.einsum("qphd,kpd->phqk", query_block, key_piece, preferred_element_type=jnp.float32)
            * score_scale
        )
        key_pos = jnp.arange(key_piece.shape[0], dtype=jnp.int32)
        allowed = key_pos[None, :] <= query_pos[:, None]
        scores = jnp.where(allowed, scores, -1e30)
        new_max = jnp.maximum(running_max, jnp.max(scores, axis=3))
        weights = jnp.where(allowed, jnp.exp(scores - new_max[..., None]), 0.0)
        running_sum = jnp.sum(weights, axis=3)
        running_acc = jnp.einsum(
            "phqk,kpd->phqd",
            weights.astype(jnp.bfloat16),
            value_piece,
            preferred_element_type=jnp.float32,
        )
        return (new_max, running_sum, running_acc)

    final_state = lax.cond(
        jnp.int32(0) <= first_query + length_here - 1,
        compute,
        lambda state_in: state_in,
        start_state,
    )
    running_max, running_sum, running_acc = final_state
    attended = (running_acc / running_sum[..., None]).astype(jnp.bfloat16)
    attended = jnp.transpose(attended, (2, 0, 1, 3)).reshape(
        length_here, pair_count, local_heads * HEAD_DIM
    )
    keep_rows = length_here // expert_size
    projected = lax.psum_scatter(
        jnp.einsum(
            "qpf,fd->qpd", attended, output_weight, preferred_element_type=jnp.float32
        ).astype(jnp.bfloat16),
        "exp",
        scatter_dimension=0,
        tiled=True,
    ).astype(jnp.float32)
    stream = (tokens.astype(jnp.float32) + projected).astype(jnp.bfloat16)
    stream_wide = stream.astype(jnp.float32)
    normed = (
        stream_wide
        * lax.rsqrt(jnp.mean(stream_wide * stream_wide, axis=2, keepdims=True) + 1e-06)
        * norm_gain.astype(jnp.float32)
    ).astype(jnp.bfloat16)
    row_count = keep_rows * pair_count
    normed_rows = normed.reshape(row_count, D)
    expert_total = expand_weight.shape[0] * context_size * expert_size
    capacity = max(2, (3 * row_count * TOP + 2 * expert_total - 1) // (2 * expert_total))
    flat_ids = routing.reshape(-1)
    one_hot = (flat_ids[:, None] == jnp.arange(expert_total, dtype=jnp.int32)[None, :]).astype(
        jnp.int32
    )
    earlier = jnp.cumsum(one_hot, axis=0) - one_hot
    slot_index = jnp.sum(earlier * one_hot, axis=1)
    destination = flat_ids * capacity + slot_index
    placement = (
        jnp.arange(expert_total * capacity, dtype=jnp.int32)[:, None] == destination[None, :]
    )
    placement = jnp.any(placement.reshape(expert_total * capacity, row_count, TOP), axis=2).astype(
        jnp.bfloat16
    )
    outgoing = jnp.dot(placement, normed_rows, preferred_element_type=jnp.float32).astype(
        jnp.bfloat16
    )
    outgoing = outgoing.reshape(expert_total, capacity, D)
    received = lax.all_to_all(outgoing, ("ctx", "exp"), split_axis=0, concat_axis=0, tiled=True)
    flat_rows = received.reshape(-1, D)
    gated = jnp.dot(flat_rows, expand_weight[0], preferred_element_type=jnp.float32)
    activated = (jax.nn.silu(gated[:, :EW]) * gated[:, EW:]).astype(jnp.bfloat16)
    expert_out = jnp.dot(activated, reduce_weight[0], preferred_element_type=jnp.float32).astype(
        jnp.bfloat16
    )
    returned = lax.all_to_all(
        expert_out.reshape(received.shape), ("ctx", "exp"), split_axis=0, concat_axis=0, tiled=True
    )
    picked = returned.reshape(expert_total * capacity, D)[destination].reshape(row_count, TOP, D)
    gate_rows = gate_values.reshape(row_count, TOP)
    mixture = jnp.einsum("rk,rkd->rd", gate_rows, picked.astype(jnp.float32))
    layer_out = (stream_wide.reshape(row_count, D) + mixture).astype(jnp.bfloat16)
    return layer_out.reshape(stream.shape)


def solution(mesh):
    in_specs = (
        P(("ctx", "exp"), None, None),
        P("ctx", None, "exp"),
        P("ctx", None, None),
        P("ctx", None, None),
        P("exp", None),
        P(),
        P(("ctx", "exp"), None, None),
        P(("ctx", "exp"), None, None),
        P(("ctx", "exp"), None, None),
        P(("ctx", "exp"), None, None),
    )
    out_specs = P(("ctx", "exp"), None, None)
    return jax.shard_map(shards, mesh=mesh, in_specs=in_specs, out_specs=out_specs, check_vma=False)
```

profile of v0, /device:TPU:1, one launch (start us, length us, event | category | flops | bytes accessed | tf_op | source)
XLA Modules:
  0.0 336.4 jit_solution(12182126572916786261)
XLA Ops:
  6.5 1.6 copy.36
  8.1 0.0 all-gather.3.cloned.1.call-update
  8.1 0.0 all-gather.5.cloned.1.call-start
  8.2 1.6 copy.37
  9.7 0.0 all-gather.5.cloned.1.call-update
  9.8 0.0 reduce-scatter.2.cloned.1.call-start
  9.8 51.3 %all-gather.3.cloned.1.call-done = bf16[2048,2,256]{2,0,1:T(8,128)(2,1)} async-done(((bf16[128,2,256]{2,0,1:T(8,128)(2,1)}), bf16[2048,2,256]{2,0,1:T(8,128)(2,1)}) %all-gather.3.cloned.1.call-update) | async-done | bytes 2097168 | tf_op jit(solution)/shard_map/all_gather | solution.py:43
  61.1 48.8 %all-gather.5.cloned.1.call-done = bf16[2048,2,256]{2,0,1:T(8,128)(2,1)} async-done(((bf16[128,2,256]{2,0,1:T(8,128)(2,1)}), bf16[2048,2,256]{2,0,1:T(8,128)(2,1)}) %all-gather.5.cloned.1.call-update) | async-done | bytes 2097168 | tf_op jit(solution)/shard_map/all_gather | solution.py:46
  110.0 8.2 %conditional.1 = (f32[2,4,128]{2,1,0:T(4,128)S(1)}, f32[2,4,128,128]{2,3,1,0:T(8,128)S(1)}) conditional(s32[]{:T(128)} %convert_element_type.57, () %tuple.34, (s32[]{:T(128)}, s32[128]{0:T(128)S(1)}, s32[]{:T(128)}, pred[]{:T(512)}, pred[]{:T(512)}, /*index=5*/s32[]{:T(128)}, bf16[2048,2,256]{2,0,1:T(8,128)(2,1)}, ...), branch_computations={%region_0.1_spmd, %region_1.4_spmd.clone} | conditional | flops 1101266048 | bytes 38037236 | solution.py:69
  110.0 0.2 iota_compare_fusion
  110.1 1.1 reshape.144
  111.3 2.7 fusion
  114.0 2.0 fusion.3
  116.1 2.0 fusion.2
  118.1 0.1 divide_convert_fusion
  118.2 4.9 %convolution_convert_fusion.1 = bf16[128,2,4096]{2,0,1:T(8,128)(2,1)} fusion(bf16[128,2,512]{0,2,1:T(8,128)(2,1)S(1)} %bitcast.73, bf16[512,4096]{1,0:T(8,128)(2,1)} %param.16), kind=kOutput, calls=%fused_computation.28 | convolution fusion | flops 1074790400 | bytes 6553600 | tf_op jit(solution)/shard_map/qpf,fd->qpd/dot_general | solution.py:82
  123.1 0.1 copy.42
  123.2 0.1 eq.44
  123.3 0.1 eq.40
  123.4 0.1 copy.44
  123.5 0.2 fusion.33
  123.8 0.2 fusion.35
  124.0 0.1 reduce_sum.37
  124.1 0.1 copy.41
  124.2 0.2 fusion.31
  124.4 34.6 %reduce-scatter.2.cloned.1.call-done = bf16[16,2,4096]{2,0,1:T(8,128)(2,1)} async-done(((bf16[128,2,4096]{2,0,1:T(8,128)(2,1)}), bf16[16,2,4096]{2,0,1:T(8,128)(2,1)}) %reduce-scatter.2.cloned.1.call-update) | async-done | bytes 262160 | tf_op jit(solution)/shard_map/reduce_scatter | solution.py:81
  159.0 1.3 multiply_reduce_fusion
  160.3 2.0 multiply_convert_fusion
  162.3 0.3 copy.46
  162.6 0.1 reshape.123
  162.7 1.0 convolution_convert_fusion
  163.7 4.4 %reshape.124 = bf16[128,3,4096]{2,1,0:T(4,128)(2,1)} reshape(bf16[384,4096]{1,0:T(8,128)(2,1)S(1)} %convolution_convert_fusion) | data formatting | bytes 6291456 | tf_op jit(solution)/shard_map/reshape | solution.py:116
  168.2 65.2 %all_to_all.10 = bf16[128,3,4096]{2,1,0:T(4,128)(2,1)} all-to-all(bf16[128,3,4096]{2,1,0:T(4,128)(2,1)} %reshape.124), channel_id=1, replica_groups=mesh['ctx'=16,'exp'=8] {'ctx','exp'}, dimensions={0} | all-to-all | bytes 6291456 | tf_op jit(solution)/shard_map/all_to_all | solution.py:117
  233.3 6.0 %reshape.125 = bf16[384,4096]{1,0:T(8,128)(2,1)S(1)} reshape(bf16[128,3,4096]{2,1,0:T(4,128)(2,1)} %all_to_all.10) | data formatting | bytes 6291456 | tf_op jit(solution)/shard_map/reshape | solution.py:118
  239.3 8.0 %fusion.17 = f32[384,1536]{1,0:T(8,128)S(1)} fusion(bf16[384,4096]{1,0:T(8,128)(2,1)S(1)} %reshape.125, bf16[1,4096,1536]{2,1,0:T(8,128)(2,1)} %param.20), kind=kOutput, calls=%fused_computation.22 | convolution fusion | flops 4831838208 | bytes 18087936 | tf_op jit(solution)/shard_map/dot_general | solution.py:119
  247.3 5.7 %fusion.21 = bf16[384,4096]{1,0:T(8,128)(2,1)S(1)} fusion(bf16[1,768,4096]{2,1,0:T(8,128)(2,1)} %param.21, f32[384,1536]{1,0:T(8,128)S(1)} %fusion.17), kind=kOutput, calls=%fused_computation.27 | convolution fusion | flops 2419261440 | bytes 11796480 | tf_op jit(solution)/shard_map/dot_general | solution.py:121
  253.1 4.5 %reshape.126 = bf16[128,3,4096]{2,1,0:T(4,128)(2,1)} reshape(bf16[384,4096]{1,0:T(8,128)(2,1)S(1)} %fusion.21) | data formatting | bytes 6291456 | tf_op jit(solution)/shard_map/reshape | solution.py:125
  257.5 6.0 %all-to-all-start.1 = ((bf16[128,3,4096]{2,1,0:T(4,128)(2,1)}), bf16[128,3,4096]{2,1,0:T(4,128)(2,1)}, u32[]{:S(2)}, u32[]{:S(2)}) async-start(bf16[128,3,4096]{2,1,0:T(4,128)(2,1)} %reshape.126), calls=%async_computation.2 | async-start | bytes 8388608 | tf_op jit(solution)/shard_map/all_to_all | solution.py:124
  263.5 0.1 mul.89
  263.6 0.1 copy.48
  263.7 0.4 copy.40
  264.1 1.2 reshape.121
  265.3 50.8 %all-to-all-done.1 = bf16[128,3,4096]{2,1,0:T(4,128)(2,1)} async-done(((bf16[128,3,4096]{2,1,0:T(4,128)(2,1)}), bf16[128,3,4096]{2,1,0:T(4,128)(2,1)}, u32[]{:S(2)}, u32[]{:S(2)}) %all-to-all-start.1) | async-done | bytes 3145760 | tf_op jit(solution)/shard_map/all_to_all | solution.py:124
  316.1 6.0 %reshape.127 = bf16[384,4096]{1,0:T(8,128)(2,1)S(1)} reshape(bf16[128,3,4096]{2,1,0:T(4,128)(2,1)} %all-to-all-done.1) | data formatting | bytes 6291456 | tf_op jit(solution)/shard_map/reshape | solution.py:127
  322.1 3.2 gather_fusion
  325.3 2.3 fusion.25
  327.6 1.4 fusion.30
  328.9 0.9 reshape.130
  (29 shorter events, 0.2 us)
Async XLA Ops:
  6.5 54.6 %all-gather.3.cloned.1.call-start = ((), (), s32[]{:S(2)}) async-start(), calls=%async_computation.3 | async-start | bytes 2228224 | tf_op jit(solution)/shard_map/all_gather | solution.py:43
  8.1 101.8 %all-gather.5.cloned.1.call-start = ((), (), s32[]{:S(2)}) async-start(), calls=%async_computation.4 | async-start | bytes 2228224 | tf_op jit(solution)/shard_map/all_gather | solution.py:46
  9.8 149.2 %reduce-scatter.2.cloned.1.call-start = ((), (), s32[]{:S(2)}) async-start(), calls=%async_computation.5 | async-start | bytes 2359296 | tf_op jit(solution)/shard_map/reduce_scatter | solution.py:81
  111.3 2.8 copy-start.5
  118.2 4.9 %copy-start.2 = (s32[16,2,8]{0,2,1:T(8,128)S(1)}, s32[16,2,8]{0,2,1:T(8,128)}, u32[]{:S(2)}) copy-start(s32[16,2,8]{0,2,1:T(8,128)} %param.18) | copy-start | bytes 3076
  118.2 5.2 %copy-start.3 = (bf16[4096]{0:T(1024)(128)(2,1)S(1)}, bf16[4096]{0:T(1024)(128)(2,1)}, u32[]{:S(2)}) copy-start(bf16[4096]{0:T(1024)(128)(2,1)} %param.17) | copy-start | bytes 24580
  118.2 40.8 %copy-start.1 = (bf16[16,2,4096]{2,1,0:T(2,128)(2,1)S(1)}, bf16[16,2,4096]{2,1,0:T(2,128)(2,1)}, u32[]{:S(2)}) copy-start(bf16[16,2,4096]{2,1,0:T(2,128)(2,1)} %param.12) | copy-start | bytes 786436
  257.5 6.1 %copy-start.4 = (f32[16,2,8]{0,2,1:T(8,128)S(1)}, f32[16,2,8]{0,2,1:T(8,128)}, u32[]{:S(2)}) copy-start(f32[16,2,8]{0,2,1:T(8,128)} %param.19) | copy-start | bytes 3076
  257.5 6.2 %copy-start = (f32[16,2,4096]{2,0,1:T(8,128)S(1)}, f32[16,2,4096]{2,0,1:T(8,128)}, u32[]{:S(2)}) copy-start(f32[16,2,4096]{2,0,1:T(8,128)} %get-tuple-element.204) | copy-start | bytes 1572868
  257.5 58.6 %all-to-all-start.1 = ((bf16[128,3,4096]{2,1,0:T(4,128)(2,1)}), bf16[128,3,4096]{2,1,0:T(4,128)(2,1)}, u32[]{:S(2)}, u32[]{:S(2)}) async-start(bf16[128,3,4096]{2,1,0:T(4,128)(2,1)} %reshape.126), calls=%async_computation.2 | async-start | bytes 8388608 | tf_op jit(solution)/shard_map/all_to_all | solution.py:124
Sparse Core Ops, SparseCore 0:
  9.8 51.2 all-gather.2
  63.6 46.3 all-gather.4
  123.2 35.7 reduce-scatter.1
where the time goes:
time: 337 us; the launch traced here: 336 us
  waiting for transfers between devices  186 us (55%)
  blocking collectives  65.2 us (19%)
  local copies, waits for them, and re-layouts  31.9 us (9%)
  matrix products  26.7 us (8%)
  between operations  13.3 us (4%)
  other arithmetic  7.61 us (2%)
  starting transfers between devices  6.05 us (2%)
    all_to_all x1, blocking collectives, shards(): lax.all_to_all(outgoing, ('ctx', 'exp'), split_axis=0, concat_axis=0, til...  65.2 us
    all_gather x1, waiting for transfers between devices, shards(): lax.all_gather(keys, 'ctx', axis=0, tiled=True)  51.3 us
    all_to_all x1, waiting for transfers between devices, shards(): lax.all_to_all(expert_out.reshape(received.shape), ('ctx', 'exp'), split_...  50.8 us
    all_gather x1, waiting for transfers between devices, shards(): lax.all_gather(values, 'ctx', axis=0, tiled=True)  48.8 us
    reduce_scatter x1, waiting for transfers between devices, shards(): lax.psum_scatter(jnp.einsum('qpf,fd->qpd', attended, output_weight, prefe...  34.6 us
    dot_general x1, matrix products, shards(): jnp.dot(flat_rows, expand_weight[0], preferred_element_type=jnp.float32)  8.01 us
  transfers between devices with their start and end apart: 4, of which 4 were waited for; matrix products, arithmetic and copies ran while one was open for 1% of the time, Pallas kernels for 0%

commit v1 on v0

v1 whole, which is shorter than its diff:
```python
import functools

import jax
import jax.numpy as jnp
from jax import lax
from jax.experimental import pallas as pl
from jax.experimental.pallas import tpu as pltpu
from jax.sharding import PartitionSpec as P

D = 4096
HEADS = 32
KV_HEADS = 2
HEAD_DIM = 128
EW = 768
TOP = 8
CAP = 3
PARTS = 8
PART = D // PARTS
LOG2E = 1.4426950408889634
F32 = jnp.float32
BF16 = jnp.bfloat16
MIB = 1 << 20


def contract(lhs, rhs, lhs_dim, rhs_dim):
    return lax.dot_general(
        lhs, rhs, (((lhs_dim,), (rhs_dim,)), ((), ())), preferred_element_type=F32
    )


def attend_kernel(pos_ref, q_ref, kv0_ref, kv1_ref, w_ref, out_ref, score_ref, *, blocks, length, pairs, heads):
    cols = heads * length
    query_pos = pos_ref[0] + lax.broadcasted_iota(jnp.int32, (length, cols), 1) % length
    key_iota = lax.broadcasted_iota(jnp.int32, (length, cols), 0)
    scale = HEAD_DIM ** (-0.5) * LOG2E
    total = 2 * blocks
    for p in range(pairs):
        query = jnp.concatenate(
            [
                q_ref[:, (p * heads + h) * HEAD_DIM : (p * heads + h + 1) * HEAD_DIM]
                for h in range(heads)
            ],
            axis=0,
        )
        top = jnp.full((1, cols), -1e30, F32)
        for b in range(total):
            source = kv0_ref if b < blocks else kv1_ref
            key = source[b % blocks, :, p * 2 * HEAD_DIM : (p * 2 + 1) * HEAD_DIM]
            score = contract(key, query, 1, 1) * scale
            score = jnp.where(key_iota + pos_ref[1 + b] <= query_pos, score, -1e30)
            score_ref[b] = score
            top = jnp.maximum(top, jnp.max(score, axis=0, keepdims=True))
        mass = jnp.zeros((1, cols), F32)
        acc = jnp.zeros((HEAD_DIM, cols), F32)
        for b in range(total):
            source = kv0_ref if b < blocks else kv1_ref
            value = source[b % blocks, :, (p * 2 + 1) * HEAD_DIM : (p * 2 + 2) * HEAD_DIM]
            weight = jnp.exp2(score_ref[b] - top)
            mass = mass + jnp.sum(weight, axis=0, keepdims=True)
            acc = acc + contract(value, weight.astype(BF16), 0, 0)
        attended = acc / mass
        attended = jnp.concatenate(
            [attended[:, h * length : (h + 1) * length].T for h in range(heads)], axis=1
        ).astype(BF16)
        groups = out_ref.shape[0]
        rows = length // groups
        step = 1024
        for n in range(0, D, step):
            part = jnp.dot(attended, w_ref[:, n : n + step], preferred_element_type=F32)
            out_ref[:, p * rows : (p + 1) * rows, n : n + step] = part.astype(BF16).reshape(
                groups, rows, step
            )


def prepare_kernel(routing_ref, gate_ref, place_ref, mix_ref):
    rows = routing_ref.shape[0]
    experts = place_ref.shape[0] // (CAP * PARTS)
    slots = place_ref.shape[0]
    width = PARTS * rows
    expert_iota = lax.broadcasted_iota(jnp.int32, (rows, experts), 1)
    named = jnp.zeros((rows, experts), F32)
    gates = jnp.zeros((rows, experts), F32)
    for k in range(TOP):
        hit = routing_ref[:, k : k + 1] == expert_iota
        named = jnp.where(hit, 1.0, named)
        gates = jnp.where(hit, gate_ref[:, k : k + 1], gates)
    lower = (
        lax.broadcasted_iota(jnp.int32, (rows, rows), 0)
        >= lax.broadcasted_iota(jnp.int32, (rows, rows), 1)
    ).astype(BF16)
    rank = named * jnp.dot(lower, named.astype(BF16), preferred_element_type=F32)
    spread = (
        lax.broadcasted_iota(jnp.int32, (rows, width), 0)
        == lax.broadcasted_iota(jnp.int32, (rows, width), 1) % rows
    ).astype(BF16)
    wide = contract(rank.astype(BF16), spread, 0, 0).astype(BF16)
    chunk = 768
    for s in range(0, slots, chunk):
        slot = s + lax.broadcasted_iota(jnp.int32, (chunk, experts), 0)
        owner = (
            slot // (CAP * PARTS) == lax.broadcasted_iota(jnp.int32, (chunk, experts), 1)
        ).astype(BF16)
        ranks = jnp.dot(owner, wide, preferred_element_type=F32)
        row = s + lax.broadcasted_iota(jnp.int32, (chunk, width), 0)
        col = lax.broadcasted_iota(jnp.int32, (chunk, width), 1)
        hit = (ranks == (row // PARTS % CAP + 1).astype(F32)) & (row % PARTS == col // rows)
        place_ref[s : s + chunk, :] = hit.astype(BF16)
        slot = s + lax.broadcasted_iota(jnp.int32, (experts, chunk), 1)
        owner = (
            slot // (CAP * PARTS) == lax.broadcasted_iota(jnp.int32, (experts, chunk), 0)
        ).astype(BF16)
        ranks = jnp.dot(rank.astype(BF16), owner, preferred_element_type=F32)
        value = jnp.dot(gates.astype(BF16), owner, preferred_element_type=F32)
        col = s + lax.broadcasted_iota(jnp.int32, (rows, chunk), 1)
        value = jnp.where(ranks == (col // PARTS % CAP + 1).astype(F32), value, 0.0)
        for c in range(PARTS):
            mix_ref[c * rows : (c + 1) * rows, s : s + chunk] = jnp.where(
                col % PARTS == c, value, 0.0
            ).astype(BF16)


def dispatch_kernel(part_ref, token_ref, gain_ref, place_ref, out_ref, stream_ref):
    sources = part_ref.shape[0]
    rows = token_ref.shape[0]
    square = jnp.zeros((rows, 1), F32)
    for c in range(PARTS):
        cols = slice(c * PART, (c + 1) * PART)
        total = part_ref[0, :, cols].astype(F32)
        for s in range(1, sources):
            total = total + part_ref[s, :, cols].astype(F32)
        stream = (token_ref[:, cols].astype(F32) + total).astype(BF16)
        stream_ref[c * rows : (c + 1) * rows, :] = stream
        wide = stream.astype(F32)
        square = square + jnp.sum(wide * wide, axis=1, keepdims=True)
    factor = lax.rsqrt(square * (1.0 / D) + 1e-06)
    normed = jnp.concatenate(
        [
            (
                stream_ref[c * rows : (c + 1) * rows, :].astype(F32)
                * factor
                * gain_ref[:, c * PART : (c + 1) * PART].astype(F32)
            ).astype(BF16)
            for c in range(PARTS)
        ],
        axis=0,
    )
    step = 384
    for s in range(0, place_ref.shape[0], step):
        out_ref[s : s + step, :] = jnp.dot(
            place_ref[s : s + step, :], normed, preferred_element_type=F32
        ).astype(BF16)


def expert_kernel(x_ref, w1_ref, w2_ref, out_ref, w1_buf, w2_buf, rows_ref, gated_ref, sem1, sem2):
    slots = rows_ref.shape[0]
    first = [
        pltpu.make_async_copy(
            w1_ref.at[pl.ds(c * PART, PART), :], w1_buf.at[pl.ds(c * PART, PART), :], sem1.at[c]
        )
        for c in range(PARTS)
    ]
    depth = EW // 3
    second = [
        pltpu.make_async_copy(
            w2_ref.at[pl.ds(j * depth, depth), :], w2_buf.at[pl.ds(j * depth, depth), :], sem2.at[j]
        )
        for j in range(3)
    ]
    for copy in first + second:
        copy.start()
    group = 32
    size = group * PARTS
    left = lax.broadcasted_iota(jnp.int32, (size, size), 0)
    right = lax.broadcasted_iota(jnp.int32, (size, size), 1)
    gather = ((left % group) * PARTS + left // group == right).astype(BF16)
    scatter = ((right % group) * PARTS + right // group == left).astype(BF16)
    for g in range(slots // group):
        moved = jnp.dot(
            gather, x_ref[g * size : (g + 1) * size, :], preferred_element_type=F32
        ).astype(BF16)
        for c in range(PARTS):
            rows_ref[g * group : (g + 1) * group, c * PART : (c + 1) * PART] = moved[
                c * group : (c + 1) * group, :
            ]
    for c in range(PARTS):
        first[c].wait()
        for n in range(0, 2 * EW, PART):
            part = jnp.dot(
                rows_ref[:, c * PART : (c + 1) * PART],
                w1_buf[c * PART : (c + 1) * PART, n : n + PART],
                preferred_element_type=F32,
            )
            if c == 0:
                gated_ref[:, n : n + PART] = part
            else:
                gated_ref[:, n : n + PART] += part
    gate = gated_ref[:, :EW]
    active = (gate / (1.0 + jnp.exp(-gate)) * gated_ref[:, EW:]).astype(BF16)
    for copy in second:
        copy.wait()
    for c in range(PARTS):
        rows_ref[:, c * PART : (c + 1) * PART] = jnp.dot(
            active, w2_buf[:, c * PART : (c + 1) * PART], preferred_element_type=F32
        ).astype(BF16)
    for g in range(slots // group):
        stacked = jnp.concatenate(
            [
                rows_ref[g * group : (g + 1) * group, c * PART : (c + 1) * PART]
                for c in range(PARTS)
            ],
            axis=0,
        )
        out_ref[g * size : (g + 1) * size, :] = jnp.dot(
            scatter, stacked, preferred_element_type=F32
        ).astype(BF16)


def combine_kernel(back_ref, mix_ref, stream_ref, out_ref):
    rows = out_ref.shape[0]
    mixture = jnp.dot(mix_ref[...], back_ref[...], preferred_element_type=F32)
    layer = (stream_ref[...].astype(F32) + mixture).astype(BF16)
    for c in range(PARTS):
        out_ref[:, c * PART : (c + 1) * PART] = layer[c * rows : (c + 1) * rows, :]


def call(kernel, outs, scratch, limit, flops, moved):
    return pl.pallas_call(
        kernel,
        out_shape=outs,
        scratch_shapes=scratch,
        compiler_params=pltpu.CompilerParams(vmem_limit_bytes=limit * MIB),
        cost_estimate=pl.CostEstimate(flops=flops, bytes_accessed=moved, transcendentals=0),
    )


def shards(
    tokens,
    queries,
    keys,
    values,
    output_weight,
    norm_gain,
    routing,
    gate_values,
    expand_weight,
    reduce_weight,
):
    length, pairs, local = queries.shape
    heads = local // HEAD_DIM
    context_size = lax.axis_size("ctx")
    expert_size = lax.axis_size("exp")
    experts = context_size * expert_size
    here = lax.axis_index("ctx")
    key_head = lax.axis_index("exp") * heads // (HEADS // KV_HEADS)
    rows = tokens.shape[0] * pairs
    slots = experts * CAP

    own = jnp.concatenate(
        [
            lax.dynamic_slice_in_dim(array, key_head * HEAD_DIM, HEAD_DIM, 2)
            for array in (keys, values)
        ],
        axis=2,
    ).reshape(length, pairs * 2 * HEAD_DIM)
    blocks = context_size // 2
    same = [[c for c in range(k, context_size, 2)] for k in range(2)]
    near = lax.all_to_all(
        jnp.broadcast_to(own[None], (blocks,) + own.shape),
        "ctx",
        0,
        0,
        axis_index_groups=same,
        tiled=True,
    )
    far = lax.ppermute(near, "ctx", [(c, c ^ 1) for c in range(context_size)])
    core = here % 2
    block = jnp.arange(blocks, dtype=jnp.int32) * 2
    positions = (
        jnp.concatenate([here[None].astype(jnp.int32), block + core, block + 1 - core]) * length
    )
    in_vmem = pl.BlockSpec(memory_space=pltpu.VMEM)
    projected = pl.pallas_call(
        functools.partial(
            attend_kernel, blocks=blocks, length=length, pairs=pairs, heads=heads
        ),
        out_shape=jax.ShapeDtypeStruct((expert_size, rows, D), BF16),
        in_specs=[pl.BlockSpec(memory_space=pltpu.SMEM)] + [in_vmem] * 4,
        out_specs=in_vmem,
        scratch_shapes=[pltpu.VMEM((2 * blocks, length, heads * length), F32)],
        compiler_params=pltpu.CompilerParams(vmem_limit_bytes=48 * MIB),
        cost_estimate=pl.CostEstimate(
            flops=2 * 10**9, bytes_accessed=9 * MIB, transcendentals=2 * 10**6
        ),
    )(positions, queries.reshape(length, pairs * local), near, far, output_weight)

    received = lax.all_to_all(projected, "exp", 0, 0, tiled=True)

    def pair_major(array):
        return jnp.swapaxes(array, 0, 1).reshape(rows, array.shape[2])

    place, mix = call(
        prepare_kernel,
        (
            jax.ShapeDtypeStruct((slots * PARTS, PARTS * rows), BF16),
            jax.ShapeDtypeStruct((PARTS * rows, slots * PARTS), BF16),
        ),
        [],
        32,
        10**9,
        3 * MIB,
    )(pair_major(routing), pair_major(gate_values))
    outgoing, stream = call(
        dispatch_kernel,
        (
            jax.ShapeDtypeStruct((slots * PARTS, PART), BF16),
            jax.ShapeDtypeStruct((PARTS * rows, PART), BF16),
        ),
        [],
        32,
        10**9,
        8 * MIB,
    )(received, pair_major(tokens), norm_gain[None], place)
    exchanged = (experts, CAP * PARTS, PART)
    arrived = lax.all_to_all(
        outgoing.reshape(exchanged), ("ctx", "exp"), 0, 0, tiled=True
    ).reshape(slots * PARTS, PART)
    anywhere = pl.BlockSpec(memory_space=pl.ANY)
    results = pl.pallas_call(
        expert_kernel,
        out_shape=jax.ShapeDtypeStruct((slots * PARTS, PART), BF16),
        in_specs=[in_vmem, anywhere, anywhere],
        out_specs=in_vmem,
        scratch_shapes=[
            pltpu.VMEM((D, 2 * EW), BF16),
            pltpu.VMEM((EW, D), BF16),
            pltpu.VMEM((slots, D), BF16),
            pltpu.VMEM((slots, 2 * EW), F32),
            pltpu.SemaphoreType.DMA((PARTS,)),
            pltpu.SemaphoreType.DMA((3,)),
        ],
        compiler_params=pltpu.CompilerParams(vmem_limit_bytes=48 * MIB),
        cost_estimate=pl.CostEstimate(
            flops=8 * 10**9, bytes_accessed=25 * MIB, transcendentals=3 * 10**5
        ),
    )(arrived, expand_weight[0], reduce_weight[0])
    returned = lax.all_to_all(
        results.reshape(exchanged), ("ctx", "exp"), 0, 0, tiled=True
    ).reshape(slots * PARTS, PART)
    layer = call(
        combine_kernel,
        jax.ShapeDtypeStruct((rows, D), BF16),
        [],
        32,
        10**9,
        5 * MIB,
    )(returned, mix, stream)
    return jnp.swapaxes(layer.reshape(pairs, tokens.shape[0], D), 0, 1)


def solution(mesh):
    in_specs = (
        P(("ctx", "exp"), None, None),
        P("ctx", None, "exp"),
        P("ctx", None, None),
        P("ctx", None, None),
        P("exp", None),
        P(),
        P(("ctx", "exp"), None, None),
        P(("ctx", "exp"), None, None),
        P(("ctx", "exp"), None, None),
        P(("ctx", "exp"), None, None),
    )
    out_specs = P(("ctx", "exp"), None, None)
    return jax.shard_map(shards, mesh=mesh, in_specs=in_specs, out_specs=out_specs, check_vma=False)
```

time: 337 us -> 184 us (0.55)
  waiting for transfers between devices: 186 us -> 24.1 us
  blocking collectives: 65.2 us -> 120 us
  matrix products: 26.7 us -> 0 us
  Pallas kernels: 0 us -> 26.6 us
  local copies, waits for them, and re-layouts: 31.9 us -> 6.16 us
  between operations: 13.3 us -> 0.14 us
  other arithmetic: 7.61 us -> 0.22 us
    all_gather x2 -> x0, waiting for transfers between devices: 100 us -> none  [the longest x1 51.3 us: shards(): lax.all_gather(keys, 'ctx', axis=0, tiled=True)]
    all_to_all x1 -> x3, blocking collectives: 65.2 us -> 120 us  [the longest x1 49.7 us: shards(): lax.all_to_all(outgoing.reshape(exchanged), ('ctx', 'exp'), 0, 0, tiled=T...]
    reduce_scatter x1 -> x0, waiting for transfers between devices: 34.6 us -> none  [shards(): lax.psum_scatter(jnp.einsum('qpf,fd->qpd', attended, output_weight, prefe...]
    all_to_all x1, waiting for transfers between devices: 50.8 us -> 21.9 us  [shards(): received = lax.all_to_all(projected, 'exp', 0, 0, tiled=True)]
    pallas_call x0 -> x5, Pallas kernels: none -> 26.6 us  [the longest x1 12.7 us: shards(): pl.pallas_call(expert_kernel, out_shape=jax.ShapeDtypeStruct((slots * PAR...]
    dot_general x6 -> x0, matrix products: 24.7 us -> none  [the longest x1 8.01 us: shards(): jnp.dot(flat_rows, expand_weight[0], preferred_element_type=jnp.float32)]
    reshape x8 -> x1, local copies, waits for them, and re-layouts: 24.1 us -> 0.98 us  [shards(): return jnp.swapaxes(layer.reshape(pairs, tokens.shape[0], D), 0, 1)]
    reduce_sum x3 -> x0, other arithmetic: 3.52 us -> none  [the longest x1 2.01 us: compute(): running_sum = jnp.sum(weights, axis=3)]
  transfers between devices with their start and end apart: 4 -> 2, of which waited for: 4 -> 2; matrix products, arithmetic and copies ran while one was open for 1% -> 0% of each run, Pallas kernels for 0% -> 1%
where the time goes in v1:
time: 184 us
  blocking collectives  120 us (65%)
  Pallas kernels  26.6 us (14%)
  waiting for transfers between devices  24.1 us (13%)
  starting transfers between devices  6.23 us (3%)
  local copies, waits for them, and re-layouts  6.16 us (3%)
    all_to_all x1, blocking collectives, shards(): lax.all_to_all(outgoing.reshape(exchanged), ('ctx', 'exp'), 0, 0, tiled=T...  49.7 us
    all_to_all x1, blocking collectives, shards(): lax.all_to_all(results.reshape(exchanged), ('ctx', 'exp'), 0, 0, tiled=True)  46 us
    all_to_all x1, blocking collectives, shards(): lax.all_to_all(jnp.broadcast_to(own[None], (blocks,) + own.shape), 'ctx',...  24.6 us
    all_to_all x1, waiting for transfers between devices, shards(): received = lax.all_to_all(projected, 'exp', 0, 0, tiled=True)  21.9 us
    pallas_call x1, Pallas kernels, shards(): pl.pallas_call(expert_kernel, out_shape=jax.ShapeDtypeStruct((slots * PAR...  12.7 us
    pallas_call x1, Pallas kernels, shards(): pl.pallas_call(functools.partial(attend_kernel, blocks=blocks, length=len...  8.98 us
    all_to_all x1, starting transfers between devices, shards(): received = lax.all_to_all(projected, 'exp', 0, 0, tiled=True)  4.36 us
    unnamed x20, local copies, waits for them, and re-layouts  3.79 us
  transfers between devices with their start and end apart: 2, of which 2 were waited for; matrix products, arithmetic and copies ran while one was open for 0% of the time, Pallas kernels for 1%

profile of v1, /device:TPU:1, one launch (start us, length us, event | category | flops | bytes accessed | tf_op | source)
XLA Modules:
  0.0 183.7 jit_solution(363937310629708333)
XLA Ops:
  0.0 0.0 copy-start.4
  0.0 1.0 constant_dynamic-slice_fusion
  1.0 0.1 pad_maximum_fusion
  1.2 0.1 broadcast_in_dim.15
  1.3 24.6 %all_to_all.20.kv0_ref = bf16[8,128,512]{2,1,0:T(8,128)(2,1)S(1)} all-to-all(bf16[8,128,512]{2,1,0:T(8,128)(2,1)S(1)} %broadcast_in_dim.15), channel_id=1, replica_groups={{0,16,32,48,64,80,96,112},{8,24,40,56,72,88,104,120},{1,17,33,49,65,81,..., dimensions={0} | all-to-all | bytes 2097152 | tf_op jit(solution)/shard_map/all_to_all | solution.py:267
  25.9 1.9 %collective-permute-start = (bf16[8,128,512]{2,1,0:T(8,128)(2,1)S(1)}, bf16[8,128,512]{2,1,0:T(8,128)(2,1)S(1)}, u32[]{:S(2)}, u32[]{:S(2)}) collective-permute-start(bf16[8,128,512]{2,1,0:T(8,128)(2,1)S(1)} %all_to_all.20.kv0_ref), channel_id=1, source_target_pairs={{0,8},{8,0},{16,24},{24,16},{32,40},{40,32},{48,56},{56,48},{64,72... | collective-permute-start | bytes 3145736 | tf_op jit(solution)/shard_map/ppermute | solution.py:275
  27.7 0.0 copy-done.4
  27.8 0.1 add_multiply_fusion.pos_ref
  27.9 2.2 %collective-permute-done.kv1_ref = bf16[8,128,512]{2,1,0:T(8,128)(2,1)S(1)} collective-permute-done((bf16[8,128,512]{2,1,0:T(8,128)(2,1)S(1)}, bf16[8,128,512]{2,1,0:T(8,128)(2,1)S(1)}, u32[]{:S(2)}, u32[]{:S(2)}) %collective-permute-start) | collective-permute-done | bytes 1048608 | tf_op jit(solution)/shard_map/ppermute | solution.py:275
  30.0 9.0 %shard_map.100 = bf16[8,32,4096]{2,1,0:T(8,128)(2,1)} custom-call(s32[17]{0:T(128)S(1)} %add_multiply_fusion.pos_ref, bf16[128,1024]{1,0:T(8,128)(2,1)S(1)} %bitcast.24, bf16[8,128,512]{2,1,0:T(8,128)(2,1)S(1)} %all_to_all.20.kv0_ref, bf16[8,128,512]{2,1,0:T(8,128)(2,1)S(1)} %collective-permute-done.kv1_ref, bf16[512,4096]{1,0:T(8,128)(2,1)} %w_ref.1), custom_call_target="tpu_custom_call" | custom-call | flops 2000000000 | bytes 9437184 | tf_op jit(solution)/shard_map/pallas_call | solution.py:282
  39.0 0.0 copy-start.6
  39.0 0.0 copy-start.7
  39.0 0.0 copy-start.8
  39.0 0.0 copy-start.5
  39.0 4.4 %all-to-all-start.1 = ((bf16[8,32,4096]{2,1,0:T(8,128)(2,1)}), bf16[8,32,4096]{2,1,0:T(8,128)(2,1)S(1)}, u32[]{:S(2)}, u32[]{:S(2)}) async-start(bf16[8,32,4096]{2,1,0:T(8,128)(2,1)} %shard_map.100), calls=%async_computation.1 | async-start | bytes 4194304 | tf_op jit(solution)/shard_map/all_to_all | solution.py:296
  43.4 0.0 copy-done.6
  43.4 0.0 copy-done.7
  43.4 0.1 copy.12
  43.5 0.0 copy-done.8
  43.5 0.1 copy.13
  43.5 0.0 copy-done.5
  43.6 0.2 copy.11
  43.7 2.5 %shard_map.101 = (bf16[3072,256]{1,0:T(8,128)(2,1)S(1)}, bf16[256,3072]{1,0:T(8,128)(2,1)S(1)}) custom-call(s32[32,8]{1,0:T(8,128)S(1)} %bitcast.27, f32[32,8]{1,0:T(8,128)S(1)} %bitcast.28), custom_call_target="tpu_custom_call" | custom-call | flops 1000000000 | bytes 3145728 | tf_op jit(solution)/shard_map/pallas_call | solution.py:301
  46.2 0.0 copy-start
  46.2 1.2 copy-done
  47.4 0.0 copy-start.2
  47.4 1.2 copy-done.2
  48.6 21.9 %all-to-all-done.1.part_ref = bf16[8,32,4096]{2,1,0:T(8,128)(2,1)S(1)} async-done(((bf16[8,32,4096]{2,1,0:T(8,128)(2,1)}), bf16[8,32,4096]{2,1,0:T(8,128)(2,1)S(1)}, u32[]{:S(2)}, u32[]{:S(2)}) %all-to-all-start.1) | async-done | bytes 2097184 | tf_op jit(solution)/shard_map/all_to_all | solution.py:296
  70.5 0.0 copy-start.3
  70.5 1.4 copy-done.3
  71.9 1.4 shard_map.102
  73.3 49.7 %all_to_all.21 = bf16[128,24,512]{2,1,0:T(8,128)(2,1)} all-to-all(bf16[128,24,512]{2,1,0:T(8,128)(2,1)S(1)} %bitcast.22), channel_id=1, replica_groups=mesh['ctx'=16,'exp'=8] {'ctx','exp'}, dimensions={0} | all-to-all | bytes 6291456 | tf_op jit(solution)/shard_map/all_to_all | solution.py:324
  123.0 12.7 %shard_map.103 = bf16[3072,512]{1,0:T(8,128)(2,1)S(1)} custom-call(bf16[3072,512]{1,0:T(8,128)(2,1)} %bitcast.29, bf16[4096,1536]{1,0:T(8,128)(2,1)} %bitcast.36, bf16[768,4096]{1,0:T(8,128)(2,1)} %bitcast.37), custom_call_target="tpu_custom_call" | custom-call | flops 8000000000 | bytes 26214400 | tf_op jit(solution)/shard_map/pallas_call | solution.py:328
  135.7 0.0 copy-start.1
  135.8 46.0 %all_to_all.22 = bf16[128,24,512]{2,1,0:T(8,128)(2,1)S(1)} all-to-all(bf16[128,24,512]{2,1,0:T(8,128)(2,1)S(1)} %bitcast.23), channel_id=1, replica_groups=mesh['ctx'=16,'exp'=8] {'ctx','exp'}, dimensions={0} | all-to-all | bytes 6291456 | tf_op jit(solution)/shard_map/all_to_all | solution.py:346
  181.8 0.0 copy-done.1
  181.8 1.0 shard_map.104
  182.7 1.0 copy.18
  (4 shorter events, 0.1 us)
Async XLA Ops:
  0.0 27.7 %copy-start.4 = (bf16[128,2,512]{2,1,0:T(2,128)(2,1)S(1)}, bf16[128,2,512]{2,1,0:T(2,128)(2,1)}, u32[]{:S(2)}) copy-start(bf16[128,2,512]{2,1,0:T(2,128)(2,1)} %param.11) | copy-start | bytes 786436
  25.9 4.2 %collective-permute-start = (bf16[8,128,512]{2,1,0:T(8,128)(2,1)S(1)}, bf16[8,128,512]{2,1,0:T(8,128)(2,1)S(1)}, u32[]{:S(2)}, u32[]{:S(2)}) collective-permute-start(bf16[8,128,512]{2,1,0:T(8,128)(2,1)S(1)} %all_to_all.20.kv0_ref), channel_id=1, source_target_pairs={{0,8},{8,0},{16,24},{24,16},{32,40},{40,32},{48,56},{56,48},{64,72... | collective-permute-start | bytes 3145736 | tf_op jit(solution)/shard_map/ppermute | solution.py:275
  39.0 4.4 %copy-start.6 = (bf16[4096]{0:T(1024)(128)(2,1)S(1)}, bf16[4096]{0:T(1024)(128)(2,1)}, u32[]{:S(2)}) copy-start(bf16[4096]{0:T(1024)(128)(2,1)} %param.15) | copy-start | bytes 24580
  39.0 4.4 %copy-start.7 = (s32[16,2,8]{0,2,1:T(8,128)S(1)}, s32[16,2,8]{0,2,1:T(8,128)}, u32[]{:S(2)}) copy-start(s32[16,2,8]{0,2,1:T(8,128)} %param.16) | copy-start | bytes 3076
  39.0 4.5 %copy-start.8 = (f32[16,2,8]{0,2,1:T(8,128)S(1)}, f32[16,2,8]{0,2,1:T(8,128)}, u32[]{:S(2)}) copy-start(f32[16,2,8]{0,2,1:T(8,128)} %param.17) | copy-start | bytes 3076
  39.0 4.6 %copy-start.5 = (bf16[16,2,4096]{2,1,0:T(2,128)(2,1)S(1)}, bf16[16,2,4096]{2,1,0:T(2,128)(2,1)}, u32[]{:S(2)}) copy-start(bf16[16,2,4096]{2,1,0:T(2,128)(2,1)} %param.10) | copy-start | bytes 786436
  39.0 31.4 %all-to-all-start.1 = ((bf16[8,32,4096]{2,1,0:T(8,128)(2,1)}), bf16[8,32,4096]{2,1,0:T(8,128)(2,1)S(1)}, u32[]{:S(2)}, u32[]{:S(2)}) async-start(bf16[8,32,4096]{2,1,0:T(8,128)(2,1)} %shard_map.100), calls=%async_computation.1 | async-start | bytes 4194304 | tf_op jit(solution)/shard_map/all_to_all | solution.py:296
  46.2 1.2 copy-start
  47.4 1.2 copy-start.2
  70.5 1.4 copy-start.3
  135.7 46.0 %copy-start.1 = (bf16[256,3072]{1,0:T(8,128)(2,1)S(1)}, bf16[256,3072]{1,0:T(8,128)(2,1)}, u32[]{:S(2)}) copy-start(bf16[256,3072]{1,0:T(8,128)(2,1)} %copy-done) | copy-start | bytes 4718596

commit v2 on v1

--- a/solution.py
+++ b/solution.py
@@ -28,48 +28,169 @@
     )
 
 
-def attend_kernel(pos_ref, q_ref, kv0_ref, kv1_ref, w_ref, out_ref, score_ref, *, blocks, length, pairs, heads):
-    cols = heads * length
-    query_pos = pos_ref[0] + lax.broadcasted_iota(jnp.int32, (length, cols), 1) % length
-    key_iota = lax.broadcasted_iota(jnp.int32, (length, cols), 0)
+def pack_kernel(info_ref, weight_ref, query_ref, out_ref, sem):
+    depth = weight_ref.shape[0]
+    width = out_ref.shape[1]
+    extra = out_ref.shape[0] - depth
+    cols = query_ref.shape[1]
+    copies = [
+        pltpu.make_async_copy(
+            weight_ref.at[:, pl.ds(pl.multiple_of(info_ref[0], width), width)],
+            out_ref.at[pl.ds(0, depth), :],
+            sem.at[0],
+        )
+    ]
+    for i in range(width // cols):
+        copies.append(
+            pltpu.make_async_copy(
+                query_ref.at[pl.ds(i * extra, extra), :],
+                out_ref.at[pl.ds(depth, extra), pl.ds(i * cols, cols)],
+                sem.at[1 + i],
+            )
+        )
+    for copy in copies:
+        copy.start()
+    for copy in copies:
+        copy.wait()
+
+
+def pieces(source, target, count, sem, first):
+    size = source.shape[0] // count
+    return [
+        pltpu.make_async_copy(
+            source.at[pl.ds(i * size, size), :],
+            target.at[pl.ds(i * size, size), :],
+            sem.at[first + i],
+        )
+        for i in range(count)
+    ]
+
+
+def attend_kernel(
+    info_ref,
+    q0_ref,
+    own_ref,
+    near_ref,
+    far_ref,
+    weight_ref,
+    side_ref,
+    expand_ref,
+    reduce_ref,
+    out_ref,
+    low_out,
+    high_out,
+    reduce_out,
+    score_ref,
+    w0_ref,
+    w1_ref,
+    q1_ref,
+    sem,
+    *,
+    pairs,
+    heads,
+):
+    length = own_ref.shape[0]
+    depth, half = w0_ref.shape
+    extra = side_ref.shape[0] - depth
+    cols = q1_ref.shape[1]
+    copies = [
+        pltpu.make_async_copy(
+            side_ref.at[pl.ds(depth, extra), pl.ds(i * cols, cols)],
+            q1_ref.at[pl.ds(i * extra, extra), :],
+            sem.at[i],
+        )
+        for i in range(half // cols)
+    ]
+    moved = len(copies)
+    copies.append(
+        pltpu.make_async_copy(
+            weight_ref.at[:, pl.ds(pl.multiple_of(info_ref[0], half), half)],
+            w0_ref,
+            sem.at[moved],
+        )
+    )
+    copies.append(
+        pltpu.make_async_copy(side_ref.at[pl.ds(0, depth), :], w1_ref, sem.at[moved + 1])
+    )
+    middle = low_out.shape[0]
+    later_copies = pieces(expand_ref.at[pl.ds(0, middle), :], low_out, 4, sem, moved + 2)
+    later_copies += pieces(expand_ref.at[pl.ds(middle, middle), :], high_out, 4, sem, moved + 6)
+    later_copies += pieces(reduce_ref, reduce_out, 4, sem, moved + 10)
+    for copy in copies + later_copies:
+        copy.start()
+    rows = heads * length
     scale = HEAD_DIM ** (-0.5) * LOG2E
-    total = 2 * blocks
-    for p in range(pairs):
-        query = jnp.concatenate(
-            [
-                q_ref[:, (p * heads + h) * HEAD_DIM : (p * heads + h + 1) * HEAD_DIM]
-                for h in range(heads)
-            ],
-            axis=0,
-        )
-        top = jnp.full((1, cols), -1e30, F32)
-        for b in range(total):
-            source = kv0_ref if b < blocks else kv1_ref
-            key = source[b % blocks, :, p * 2 * HEAD_DIM : (p * 2 + 1) * HEAD_DIM]
-            score = contract(key, query, 1, 1) * scale
-            score = jnp.where(key_iota + pos_ref[1 + b] <= query_pos, score, -1e30)
-            score_ref[b] = score
-            top = jnp.maximum(top, jnp.max(score, axis=0, keepdims=True))
-        mass = jnp.zeros((1, cols), F32)
-        acc = jnp.zeros((HEAD_DIM, cols), F32)
-        for b in range(total):
-            source = kv0_ref if b < blocks else kv1_ref
-            value = source[b % blocks, :, (p * 2 + 1) * HEAD_DIM : (p * 2 + 2) * HEAD_DIM]
-            weight = jnp.exp2(score_ref[b] - top)
-            mass = mass + jnp.sum(weight, axis=0, keepdims=True)
-            acc = acc + contract(value, weight.astype(BF16), 0, 0)
-        attended = acc / mass
-        attended = jnp.concatenate(
-            [attended[:, h * length : (h + 1) * length].T for h in range(heads)], axis=1
-        ).astype(BF16)
-        groups = out_ref.shape[0]
-        rows = length // groups
-        step = 1024
-        for n in range(0, D, step):
-            part = jnp.dot(attended, w_ref[:, n : n + step], preferred_element_type=F32)
-            out_ref[:, p * rows : (p + 1) * rows, n : n + step] = part.astype(BF16).reshape(
-                groups, rows, step
+    later = lax.broadcasted_iota(jnp.int32, (rows, length), 1) > (
+        lax.broadcasted_iota(jnp.int32, (rows, length), 0) % length
+    )
+    span = 4 * length
+    chunks = [
+        (ref, start) for ref in (near_ref, far_ref) for start in range(0, ref.shape[0], span)
+    ]
+    groups = out_ref.shape[0]
+    keep = length // groups
+    stacked = []
+    for q_ref in (q0_ref, q1_ref):
+        if q_ref is q1_ref:
+            for copy in copies[:moved]:
+                copy.wait()
+        attended = []
+        for p in range(pairs):
+            keys = slice(p * 2 * HEAD_DIM, (p * 2 + 1) * HEAD_DIM)
+            values = slice((p * 2 + 1) * HEAD_DIM, (p * 2 + 2) * HEAD_DIM)
+            first = p * heads * HEAD_DIM
+            query = jnp.concatenate(
+                [
+                    q_ref[:, first + h * HEAD_DIM : first + (h + 1) * HEAD_DIM]
+                    for h in range(heads)
+                ],
+                axis=0,
             )
+            score = jnp.where(later, -1e30, contract(query, own_ref[:, keys], 1, 1))
+            score_ref[:, :length] = score
+            peak = score
+            for i, (ref, start) in enumerate(chunks):
+                score = contract(query, ref[start : start + span, keys], 1, 1)
+                for j in range(0, span, length):
+                    earlier = info_ref[1 + (i * span + j) // length] > 0
+                    part = jnp.where(earlier, score[:, j : j + length], -1e30)
+                    at = length + i * span + j
+                    score_ref[:, at : at + length] = part
+                    peak = jnp.maximum(peak, part)
+            peak = jnp.max(peak, axis=1, keepdims=True)
+            weight = jnp.exp2((score_ref[:, :length] - peak) * scale)
+            mass = weight
+            acc = jnp.dot(weight.astype(BF16), own_ref[:, values], preferred_element_type=F32)
+            for i, (ref, start) in enumerate(chunks):
+                at = length + i * span
+                weight = jnp.exp2((score_ref[:, at : at + span] - peak) * scale)
+                for j in range(0, span, length):
+                    mass = mass + weight[:, j : j + length]
+                acc = acc + jnp.dot(
+                    weight.astype(BF16),
+                    ref[start : start + span, values],
+                    preferred_element_type=F32,
+                )
+            acc = (acc / jnp.sum(mass, axis=1, keepdims=True)).astype(BF16)
+            attended.append(
+                jnp.concatenate(
+                    [acc[h * length : (h + 1) * length] for h in range(heads)], axis=1
+                )
+            )
+        stacked.append(jnp.concatenate(attended, axis=0))
+    for copy in copies[moved:]:
+        copy.wait()
+    step = half // 4
+    for n in range(0, half, step):
+        part = jnp.dot(stacked[0], w0_ref[:, n : n + step], preferred_element_type=F32)
+        part = part + jnp.dot(stacked[1], w1_ref[:, n : n + step], preferred_element_type=F32)
+        part = part.astype(BF16)
+        for p in range(pairs):
+            out_ref[:, p * keep : (p + 1) * keep, n : n + step] = part[
+                p * length : (p + 1) * length
+            ].reshape(groups, keep, step)
+    for copy in later_copies:
+        copy.wait()
 
 
 def prepare_kernel(routing_ref, gate_ref, place_ref, mix_ref):
@@ -119,16 +240,20 @@
             ).astype(BF16)
 
 
-def dispatch_kernel(part_ref, token_ref, gain_ref, place_ref, out_ref, stream_ref):
+def dispatch_kernel(
+    part_ref, token_ref, gain_ref, place_ref, out_ref, stream_ref
+):
     sources = part_ref.shape[0]
     rows = token_ref.shape[0]
+    half = PARTS // 2
     square = jnp.zeros((rows, 1), F32)
     for c in range(PARTS):
-        cols = slice(c * PART, (c + 1) * PART)
-        total = part_ref[0, :, cols].astype(F32)
-        for s in range(1, sources):
-            total = total + part_ref[s, :, cols].astype(F32)
-        stream = (token_ref[:, cols].astype(F32) + total).astype(BF16)
+        at = slice(c % half * PART, (c % half + 1) * PART)
+        total = token_ref[:, c * PART : (c + 1) * PART].astype(F32)
+        total = total + sum(
+            part_ref[s, :, at].astype(F32) for s in range(c // half, sources, 2)
+        )
+        stream = total.astype(BF16)
         stream_ref[c * rows : (c + 1) * rows, :] = stream
         wide = stream.astype(F32)
         square = square + jnp.sum(wide * wide, axis=1, keepdims=True)
@@ -151,23 +276,8 @@
         ).astype(BF16)
 
 
-def expert_kernel(x_ref, w1_ref, w2_ref, out_ref, w1_buf, w2_buf, rows_ref, gated_ref, sem1, sem2):
+def expert_kernel(x_ref, low_ref, high_ref, w2_ref, out_ref, rows_ref, gated_ref):
     slots = rows_ref.shape[0]
-    first = [
-        pltpu.make_async_copy(
-            w1_ref.at[pl.ds(c * PART, PART), :], w1_buf.at[pl.ds(c * PART, PART), :], sem1.at[c]
-        )
-        for c in range(PARTS)
-    ]
-    depth = EW // 3
-    second = [
-        pltpu.make_async_copy(
-            w2_ref.at[pl.ds(j * depth, depth), :], w2_buf.at[pl.ds(j * depth, depth), :], sem2.at[j]
-        )
-        for j in range(3)
-    ]
-    for copy in first + second:
-        copy.start()
     group = 32
     size = group * PARTS
     left = lax.broadcasted_iota(jnp.int32, (size, size), 0)
@@ -183,11 +293,12 @@
                 c * group : (c + 1) * group, :
             ]
     for c in range(PARTS):
-        first[c].wait()
+        half_ref = low_ref if c < PARTS // 2 else high_ref
+        at = c * PART % half_ref.shape[0]
         for n in range(0, 2 * EW, PART):
             part = jnp.dot(
                 rows_ref[:, c * PART : (c + 1) * PART],
-                w1_buf[c * PART : (c + 1) * PART, n : n + PART],
+                half_ref[at : at + PART, n : n + PART],
                 preferred_element_type=F32,
             )
             if c == 0:
@@ -196,11 +307,9 @@
                 gated_ref[:, n : n + PART] += part
     gate = gated_ref[:, :EW]
     active = (gate / (1.0 + jnp.exp(-gate)) * gated_ref[:, EW:]).astype(BF16)
-    for copy in second:
-        copy.wait()
     for c in range(PARTS):
         rows_ref[:, c * PART : (c + 1) * PART] = jnp.dot(
-            active, w2_buf[:, c * PART : (c + 1) * PART], preferred_element_type=F32
+            active, w2_ref[:, c * PART : (c + 1) * PART], preferred_element_type=F32
         ).astype(BF16)
     for g in range(slots // group):
         stacked = jnp.concatenate(
@@ -263,6 +372,30 @@
         axis=2,
     ).reshape(length, pairs * 2 * HEAD_DIM)
     blocks = context_size // 2
+    core = here % 2
+    side = lax.axis_index("exp") % 2
+    swap_core = [(c, c ^ 1) for c in range(context_size)]
+    swap_side = [
+        (c * expert_size + e, c * expert_size + (e ^ (1 + 2 * (c % 2))))
+        for c in range(context_size)
+        for e in range(expert_size)
+    ]
+    hbm_weight = pltpu.with_memory_space_constraint(output_weight, pltpu.HBM)
+    half = D // 2
+    query = queries.reshape(length, pairs * local)
+    in_vmem = pl.BlockSpec(memory_space=pltpu.VMEM)
+    anywhere = pl.BlockSpec(memory_space=pl.ANY)
+    in_smem = pl.BlockSpec(memory_space=pltpu.SMEM)
+    sent = pl.pallas_call(
+        pack_kernel,
+        out_shape=pltpu.VMEM((local + length * pairs * local // half, half), BF16),
+        in_specs=[in_smem, pl.BlockSpec(memory_space=pltpu.HBM), anywhere],
+        out_specs=in_vmem,
+        scratch_shapes=[pltpu.SemaphoreType.DMA((1 + half // (pairs * local),))],
+        compiler_params=pltpu.CompilerParams(vmem_limit_bytes=4 * MIB),
+        cost_estimate=pl.CostEstimate(flops=0, bytes_accessed=5 * MIB, transcendentals=0),
+    )(((1 - side) * half).astype(jnp.int32)[None], hbm_weight, query)
+    from_side = lax.ppermute(sent, ("ctx", "exp"), swap_side)
     same = [[c for c in range(k, context_size, 2)] for k in range(2)]
     near = lax.all_to_all(
         jnp.broadcast_to(own[None], (blocks,) + own.shape),
@@ -272,77 +405,99 @@
         axis_index_groups=same,
         tiled=True,
     )
-    far = lax.ppermute(near, "ctx", [(c, c ^ 1) for c in range(context_size)])
-    core = here % 2
+    far = lax.ppermute(near, "ctx", swap_core)
     block = jnp.arange(blocks, dtype=jnp.int32) * 2
-    positions = (
-        jnp.concatenate([here[None].astype(jnp.int32), block + core, block + 1 - core]) * length
-    )
-    in_vmem = pl.BlockSpec(memory_space=pltpu.VMEM)
-    projected = pl.pallas_call(
-        functools.partial(
-            attend_kernel, blocks=blocks, length=length, pairs=pairs, heads=heads
-        ),
-        out_shape=jax.ShapeDtypeStruct((expert_size, rows, D), BF16),
-        in_specs=[pl.BlockSpec(memory_space=pltpu.SMEM)] + [in_vmem] * 4,
-        out_specs=in_vmem,
-        scratch_shapes=[pltpu.VMEM((2 * blocks, length, heads * length), F32)],
-        compiler_params=pltpu.CompilerParams(vmem_limit_bytes=48 * MIB),
-        cost_estimate=pl.CostEstimate(
-            flops=2 * 10**9, bytes_accessed=9 * MIB, transcendentals=2 * 10**6
-        ),
-    )(positions, queries.reshape(length, pairs * local), near, far, output_weight)
-
-    received = lax.all_to_all(projected, "exp", 0, 0, tiled=True)
-
+    order = jnp.concatenate([block + core, block + 1 - core])
+    info = jnp.concatenate(
+        [(side * half).astype(jnp.int32)[None], (order < here).astype(jnp.int32)]
+    )
     def pair_major(array):
         return jnp.swapaxes(array, 0, 1).reshape(rows, array.shape[2])
 
     place, mix = call(
         prepare_kernel,
         (
-            jax.ShapeDtypeStruct((slots * PARTS, PARTS * rows), BF16),
+            pltpu.VMEM((slots * PARTS, PARTS * rows), BF16),
             jax.ShapeDtypeStruct((PARTS * rows, slots * PARTS), BF16),
         ),
         [],
-        32,
+        8,
         10**9,
         3 * MIB,
     )(pair_major(routing), pair_major(gate_values))
-    outgoing, stream = call(
+    token_rows, gain = pair_major(tokens), norm_gain[None]
+    info, place, mix, token_rows, gain = lax.optimization_barrier(
+        (info, place, mix, token_rows, gain)
+    )
+    in_hbm = pl.BlockSpec(memory_space=pltpu.HBM)
+    projected, low, high, reduce = pl.pallas_call(
+        functools.partial(attend_kernel, pairs=pairs, heads=heads),
+        out_shape=(
+            jax.ShapeDtypeStruct((expert_size, rows, half), BF16),
+            pltpu.VMEM((D // 2, 2 * EW), BF16),
+            pltpu.VMEM((D // 2, 2 * EW), BF16),
+            pltpu.VMEM((EW, D), BF16),
+        ),
+        in_specs=[in_smem] + [in_vmem] * 4 + [in_hbm, anywhere, in_hbm, in_hbm],
+        out_specs=(in_vmem,) * 4,
+        scratch_shapes=[
+            pltpu.VMEM((heads * length, (context_size + 1) * length), F32),
+            pltpu.VMEM((local, half), BF16),
+            pltpu.VMEM((local, half), BF16),
+            pltpu.VMEM((length, pairs * local), BF16),
+            pltpu.SemaphoreType.DMA((16,)),
+        ],
+        compiler_params=pltpu.CompilerParams(vmem_limit_bytes=16 * MIB),
+        cost_estimate=pl.CostEstimate(
+            flops=3 * 10**9, bytes_accessed=9 * MIB, transcendentals=4 * 10**6
+        ),
+    )(
+        info,
+        query,
+        own,
+        near.reshape(blocks * length, -1),
+        far.reshape(blocks * length, -1),
+        hbm_weight,
+        from_side,
+        pltpu.with_memory_space_constraint(expand_weight[0], pltpu.HBM),
+        pltpu.with_memory_space_constraint(reduce_weight[0], pltpu.HBM),
+    )
+
+    received = lax.all_to_all(projected, "exp", 0, 0, tiled=True)
+
+    outgoing, stream = pl.pallas_call(
         dispatch_kernel,
-        (
+        out_shape=(
             jax.ShapeDtypeStruct((slots * PARTS, PART), BF16),
             jax.ShapeDtypeStruct((PARTS * rows, PART), BF16),
         ),
-        [],
-        32,
-        10**9,
-        8 * MIB,
-    )(received, pair_major(tokens), norm_gain[None], place)
+        in_specs=[in_vmem] * 4,
+        out_specs=(in_vmem, in_vmem),
+        compiler_params=pltpu.CompilerParams(vmem_limit_bytes=8 * MIB),
+        cost_estimate=pl.CostEstimate(
+            flops=10**9, bytes_accessed=7 * MIB, transcendentals=0
+        ),
+    )(received, token_rows, gain, pltpu.with_memory_space_constraint(place, pltpu.VMEM))
     exchanged = (experts, CAP * PARTS, PART)
     arrived = lax.all_to_all(
         outgoing.reshape(exchanged), ("ctx", "exp"), 0, 0, tiled=True
     ).reshape(slots * PARTS, PART)
-    anywhere = pl.BlockSpec(memory_space=pl.ANY)
     results = pl.pallas_call(
         expert_kernel,
         out_shape=jax.ShapeDtypeStruct((slots * PARTS, PART), BF16),
-        in_specs=[in_vmem, anywhere, anywhere],
+        in_specs=[in_vmem] * 4,
         out_specs=in_vmem,
-        scratch_shapes=[
-            pltpu.VMEM((D, 2 * EW), BF16),
-            pltpu.VMEM((EW, D), BF16),
-            pltpu.VMEM((slots, D), BF16),
-            pltpu.VMEM((slots, 2 * EW), F32),
-            pltpu.SemaphoreType.DMA((PARTS,)),
-            pltpu.SemaphoreType.DMA((3,)),
-        ],
-        compiler_params=pltpu.CompilerParams(vmem_limit_bytes=48 * MIB),
+        scratch_shapes=[pltpu.VMEM((slots, D), BF16), pltpu.VMEM((slots, 2 * EW), F32)],
+        compiler_params=pltpu.CompilerParams(vmem_limit_bytes=10 * MIB),
         cost_estimate=pl.CostEstimate(
-            flops=8 * 10**9, bytes_accessed=25 * MIB, transcendentals=3 * 10**5
+            flops=8 * 10**9, bytes_accessed=6 * MIB, transcendentals=3 * 10**5
         ),
-    )(arrived, expand_weight[0], reduce_weight[0])
+    )(
+        arrived,
+        pltpu.with_memory_space_constraint(low, pltpu.VMEM),
+        pltpu.with_memory_space_constraint(high, pltpu.VMEM),
+        pltpu.with_memory_space_constraint(reduce, pltpu.VMEM),
+    )
     returned = lax.all_to_all(
         results.reshape(exchanged), ("ctx", "exp"), 0, 0, tiled=True
     ).reshape(slots * PARTS, PART)
@@ -350,7 +505,7 @@
         combine_kernel,
         jax.ShapeDtypeStruct((rows, D), BF16),
         [],
-        32,
+        8,
         10**9,
         5 * MIB,
     )(returned, mix, stream)

time: 184 us -> 174 us (0.946)
  waiting for transfers between devices: 24.1 us -> 0.01 us
  blocking collectives: 120 us -> 139 us
  local copies, waits for them, and re-layouts: 6.16 us -> 2.49 us
  starting transfers between devices: 6.23 us -> 4.13 us
    all_to_all x1 -> x0, waiting for transfers between devices: 21.9 us -> none  [shards(): received = lax.all_to_all(projected, 'exp', 0, 0, tiled=True)]
    all_to_all x0 -> x1, blocking collectives: none -> 17.1 us  [shards(): received = lax.all_to_all(projected, 'exp', 0, 0, tiled=True)]
    pallas_call x4 -> x5, Pallas kernels: 13.9 us -> 18.7 us  [the longest x1 10.8 us: shards(): pl.pallas_call(functools.partial(attend_kernel, pairs=pairs, heads=heads)...]
    all_to_all x1 -> x0, starting transfers between devices: 4.36 us -> none  [shards(): received = lax.all_to_all(projected, 'exp', 0, 0, tiled=True)]
    pallas_call x1, Pallas kernels: 12.7 us -> 9.37 us  [shards(): pl.pallas_call(expert_kernel, out_shape=jax.ShapeDtypeStruct((slots * PAR...]
    unnamed x20 -> x14, local copies, waits for them, and re-layouts: 3.79 us -> 1.03 us
    ppermute x1 -> x2, starting transfers between devices: 1.87 us -> 4.13 us  [the longest x1 3.39 us: shards(): from_side = lax.ppermute(sent, ('ctx', 'exp'), swap_side)]
    ppermute x1 -> x2, waiting for transfers between devices: 2.15 us -> 0.01 us  [the longest x1 0.01 us: shards(): far = lax.ppermute(near, 'ctx', swap_core)]
  transfers between devices with their start and end apart: 2 -> 2, of which waited for: 2 -> 0; matrix products, arithmetic and copies ran while one was open for 0% -> 0% of each run, Pallas kernels for 1% -> 1%
where the time goes in v2:
time: 174 us
  blocking collectives  139 us (80%)
  Pallas kernels  28.1 us (16%)
  starting transfers between devices  4.13 us (2%)
  local copies, waits for them, and re-layouts  2.49 us (1%)
    all_to_all x1, blocking collectives, shards(): lax.all_to_all(outgoing.reshape(exchanged), ('ctx', 'exp'), 0, 0, tiled=T...  50.9 us
    all_to_all x1, blocking collectives, shards(): lax.all_to_all(results.reshape(exchanged), ('ctx', 'exp'), 0, 0, tiled=True)  45.9 us
    all_to_all x1, blocking collectives, shards(): lax.all_to_all(jnp.broadcast_to(own[None], (blocks,) + own.shape), 'ctx',...  24.9 us
    all_to_all x1, blocking collectives, shards(): received = lax.all_to_all(projected, 'exp', 0, 0, tiled=True)  17.1 us
    pallas_call x1, Pallas kernels, shards(): pl.pallas_call(functools.partial(attend_kernel, pairs=pairs, heads=heads)...  10.8 us
    pallas_call x1, Pallas kernels, shards(): pl.pallas_call(expert_kernel, out_shape=jax.ShapeDtypeStruct((slots * PAR...  9.37 us
  transfers between devices with their start and end apart: 2, of which 0 were waited for; matrix products, arithmetic and copies ran while one was open for 0% of the time, Pallas kernels for 1%

profile of v2, /device:TPU:1, one launch (start us, length us, event | category | flops | bytes accessed | tf_op | source)
XLA Modules:
  0.0 174.0 jit_solution(16790958964898786790)
XLA Ops:
  0.0 1.0 copy.15
  1.0 0.0 copy-start.1
  1.0 0.0 copy-start.2
  1.0 3.1 %shard_map.101 = bf16[576,2048]{1,0:T(8,128)(2,1)} custom-call(s32[1]{0:T(128)} %bitcast.9.info_ref, bf16[512,4096]{1,0:T(8,128)(2,1)} %weight_ref.3, bf16[128,1024]{1,0:T(8,128)(2,1)S(1)} %bitcast.29), custom_call_target="tpu_custom_call" | custom-call | bytes 5242880 | tf_op jit(solution)/shard_map/pallas_call | solution.py:389
  4.1 0.0 copy-start.3
  4.1 0.0 copy-start.4
  4.1 0.0 copy-start.5
  4.1 0.0 copy-start
  4.2 3.4 %collective-permute-start.1 = (bf16[576,2048]{1,0:T(8,128)(2,1)}, bf16[576,2048]{1,0:T(8,128)(2,1)}, u32[]{:S(2)}, u32[]{:S(2)}) collective-permute-start(bf16[576,2048]{1,0:T(8,128)(2,1)} %shard_map.101), channel_id=1, source_target_pairs={{0,1},{1,0},{2,3},{3,2},{4,5},{5,4},{6,7},{7,6},{8,11},{9,10},{10,... | collective-permute-start | bytes 7077896 | tf_op jit(solution)/shard_map/ppermute | solution.py:398
  7.5 0.0 copy-done.1
  7.5 0.0 copy-done.2
  7.5 0.1 constant_dynamic-slice_fusion
  7.6 0.1 pad_maximum_fusion
  7.8 0.1 broadcast_in_dim.16
  7.9 24.9 %all_to_all.20 = bf16[8,128,512]{2,1,0:T(8,128)(2,1)S(1)} all-to-all(bf16[8,128,512]{2,1,0:T(8,128)(2,1)S(1)} %broadcast_in_dim.16), channel_id=1, replica_groups={{0,16,32,48,64,80,96,112},{8,24,40,56,72,88,104,120},{1,17,33,49,65,81,..., dimensions={0} | all-to-all | bytes 2097152 | tf_op jit(solution)/shard_map/all_to_all | solution.py:400
  32.8 0.7 collective-permute-start
  33.5 0.0 copy-done.3
  33.5 0.0 copy-done.4
  33.5 0.1 copy.11
  33.6 0.0 copy-done.5
  33.6 0.1 copy.12
  33.7 0.0 copy-done
  33.7 0.2 copy.13
  33.9 2.5 %shard_map.100 = (bf16[3072,256]{1,0:T(8,128)(2,1)S(1)}, bf16[256,3072]{1,0:T(8,128)(2,1)S(1)}) custom-call(s32[32,8]{1,0:T(8,128)S(1)} %bitcast.36, f32[32,8]{1,0:T(8,128)S(1)} %bitcast.37), custom_call_target="tpu_custom_call" | custom-call | flops 1000000000 | bytes 3145728 | tf_op jit(solution)/shard_map/pallas_call | solution.py:417
  36.4 0.1 compare_convert_fusion
  36.5 0.1 pad_add_fusion.info_ref
  36.6 0.0 collective-permute-done
  36.6 0.0 collective-permute-done.1.side_ref
  36.6 10.8 %shard_map.102 = (bf16[8,32,2048]{2,1,0:T(8,128)(2,1)S(1)}, bf16[2048,1536]{1,0:T(8,128)(2,1)S(1)}, bf16[2048,1536]{1,0:T(8,128)(2,1)S(1)}, bf16[768,4096]{1,0:T(8,128)(2,1)S(1)}) custom-call(s32[17]{0:T(128)S(1)} %pad_add_fusion.info_ref, bf16[128,1024]{1,0:T(8,128)(2,1)S(1)} %bitcast.30, bf16[128,512]{1,0:T(8,128)(2,1)S(1)} %bitcast.32, ...), custom_call_target="tpu_custom_call" | custom-call | flops 3000000000 | bytes 9437184 | tf_op jit(solution)/shard_map/pallas_call | solution.py:433
  47.4 17.1 %all_to_all.21.part_ref = bf16[8,32,2048]{2,1,0:T(8,128)(2,1)S(1)} all-to-all(bf16[8,32,2048]{2,1,0:T(8,128)(2,1)S(1)} %get-tuple-element.21), channel_id=1, replica_groups=mesh['ctx'=16,'exp'=8] {'exp'}, dimensions={0} | all-to-all | bytes 2097152 | tf_op jit(solution)/shard_map/all_to_all | solution.py:466
  64.5 1.3 shard_map.103
  65.8 50.9 %all_to_all.22 = bf16[128,24,512]{2,1,0:T(8,128)(2,1)S(1)} all-to-all(bf16[128,24,512]{2,1,0:T(8,128)(2,1)S(1)} %bitcast.26), channel_id=1, replica_groups=mesh['ctx'=16,'exp'=8] {'ctx','exp'}, dimensions={0} | all-to-all | bytes 6291456 | tf_op jit(solution)/shard_map/all_to_all | solution.py:482
  116.8 9.4 %shard_map.104 = bf16[3072,512]{1,0:T(8,128)(2,1)S(1)} custom-call(bf16[3072,512]{1,0:T(8,128)(2,1)S(1)} %bitcast.27, bf16[2048,1536]{1,0:T(8,128)(2,1)S(1)} %get-tuple-element.26.low_ref, bf16[2048,1536]{1,0:T(8,128)(2,1)S(1)} %get-tuple-element.27.high_ref, bf16[768,4096]{1,0:T(8,128)(2,1)S(1)} %get-tuple-element.28.w2_ref), custom_call_target="tpu_custom_call" | custom-call | flops 8000000000 | bytes 6291456 | tf_op jit(solution)/shard_map/pallas_call | solution.py:485
  126.1 45.9 %all_to_all.23 = bf16[128,24,512]{2,1,0:T(8,128)(2,1)S(1)} all-to-all(bf16[128,24,512]{2,1,0:T(8,128)(2,1)S(1)} %bitcast.28), channel_id=1, replica_groups=mesh['ctx'=16,'exp'=8] {'ctx','exp'}, dimensions={0} | all-to-all | bytes 6291456 | tf_op jit(solution)/shard_map/all_to_all | solution.py:501
  172.0 1.0 shard_map.105
  173.0 1.0 copy.18
  (3 shorter events, 0.0 us)
Async XLA Ops:
  1.0 6.6 %copy-start.1 = (bf16[128,2,256]{2,1,0:T(2,128)(2,1)S(1)}, bf16[128,2,256]{2,1,0:T(2,128)(2,1)}, u32[]{:S(2)}) copy-start(bf16[128,2,256]{2,1,0:T(2,128)(2,1)} %param.13) | copy-start | bytes 393220
  1.0 6.5 %copy-start.2 = (bf16[128,2,256]{2,1,0:T(2,128)(2,1)S(1)}, bf16[128,2,256]{2,1,0:T(2,128)(2,1)}, u32[]{:S(2)}) copy-start(bf16[128,2,256]{2,1,0:T(2,128)(2,1)} %param.12) | copy-start | bytes 393220
  4.1 29.4 %copy-start.3 = (bf16[4096]{0:T(1024)(128)(2,1)S(1)}, bf16[4096]{0:T(1024)(128)(2,1)}, u32[]{:S(2)}) copy-start(bf16[4096]{0:T(1024)(128)(2,1)} %param.15) | copy-start | bytes 24580
  4.1 29.4 %copy-start.4 = (s32[16,2,8]{0,2,1:T(8,128)S(1)}, s32[16,2,8]{0,2,1:T(8,128)}, u32[]{:S(2)}) copy-start(s32[16,2,8]{0,2,1:T(8,128)} %param.16) | copy-start | bytes 3076
  4.1 29.5 %copy-start.5 = (f32[16,2,8]{0,2,1:T(8,128)S(1)}, f32[16,2,8]{0,2,1:T(8,128)}, u32[]{:S(2)}) copy-start(f32[16,2,8]{0,2,1:T(8,128)} %param.17) | copy-start | bytes 3076
  4.1 29.6 %copy-start = (bf16[16,2,4096]{2,1,0:T(2,128)(2,1)S(1)}, bf16[16,2,4096]{2,1,0:T(2,128)(2,1)}, u32[]{:S(2)}) copy-start(bf16[16,2,4096]{2,1,0:T(2,128)(2,1)} %param.10) | copy-start | bytes 786436
  4.2 32.4 %collective-permute-start.1 = (bf16[576,2048]{1,0:T(8,128)(2,1)}, bf16[576,2048]{1,0:T(8,128)(2,1)}, u32[]{:S(2)}, u32[]{:S(2)}) collective-permute-start(bf16[576,2048]{1,0:T(8,128)(2,1)} %shard_map.101), channel_id=1, source_target_pairs={{0,1},{1,0},{2,3},{3,2},{4,5},{5,4},{6,7},{7,6},{8,11},{9,10},{10,... | collective-permute-start | bytes 7077896 | tf_op jit(solution)/shard_map/ppermute | solution.py:398
  32.8 3.8 %collective-permute-start = (bf16[8,128,512]{2,1,0:T(8,128)(2,1)S(1)}, bf16[8,128,512]{2,1,0:T(8,128)(2,1)S(1)}, u32[]{:S(2)}, u32[]{:S(2)}) collective-permute-start(bf16[8,128,512]{2,1,0:T(8,128)(2,1)S(1)} %all_to_all.20), channel_id=1, source_target_pairs={{0,8},{8,0},{16,24},{24,16},{32,40},{40,32},{48,56},{56,48},{64,72... | collective-permute-start | bytes 3145736 | tf_op jit(solution)/shard_map/ppermute | solution.py:408

commit v3 on v2

--- a/solution.py
+++ b/solution.py
@@ -28,32 +28,6 @@
     )
 
 
-def pack_kernel(info_ref, weight_ref, query_ref, out_ref, sem):
-    depth = weight_ref.shape[0]
-    width = out_ref.shape[1]
-    extra = out_ref.shape[0] - depth
-    cols = query_ref.shape[1]
-    copies = [
-        pltpu.make_async_copy(
-            weight_ref.at[:, pl.ds(pl.multiple_of(info_ref[0], width), width)],
-            out_ref.at[pl.ds(0, depth), :],
-            sem.at[0],
-        )
-    ]
-    for i in range(width // cols):
-        copies.append(
-            pltpu.make_async_copy(
-                query_ref.at[pl.ds(i * extra, extra), :],
-                out_ref.at[pl.ds(depth, extra), pl.ds(i * cols, cols)],
-                sem.at[1 + i],
-            )
-        )
-    for copy in copies:
-        copy.start()
-    for copy in copies:
-        copy.wait()
-
-
 def pieces(source, target, count, sem, first):
     size = source.shape[0] // count
     return [
@@ -66,6 +40,27 @@
     ]
 
 
+def pack_kernel(info_ref, weight_ref, query_ref, out_ref, sem):
+    depth = weight_ref.shape[0]
+    width = out_ref.shape[1]
+    extra = out_ref.shape[0] - depth
+    cols = query_ref.shape[1]
+    columns = weight_ref.at[:, pl.ds(pl.multiple_of(info_ref[0], width), width)]
+    copies = pieces(columns, out_ref.at[pl.ds(0, depth), :], 8, sem, 0)
+    for i in range(width // cols):
+        copies.append(
+            pltpu.make_async_copy(
+                query_ref.at[pl.ds(i * extra, extra), :],
+                out_ref.at[pl.ds(depth, extra), pl.ds(i * cols, cols)],
+                sem.at[8 + i],
+            )
+        )
+    for copy in copies:
+        copy.start()
+    for copy in copies:
+        copy.wait()
+
+
 def attend_kernel(
     info_ref,
     q0_ref,
@@ -74,13 +69,9 @@
     far_ref,
     weight_ref,
     side_ref,
-    expand_ref,
-    reduce_ref,
     out_ref,
-    low_out,
-    high_out,
-    reduce_out,
     score_ref,
+    bias_ref,
     w0_ref,
     w1_ref,
     q1_ref,
@@ -112,21 +103,24 @@
     copies.append(
         pltpu.make_async_copy(side_ref.at[pl.ds(0, depth), :], w1_ref, sem.at[moved + 1])
     )
-    middle = low_out.shape[0]
-    later_copies = pieces(expand_ref.at[pl.ds(0, middle), :], low_out, 4, sem, moved + 2)
-    later_copies += pieces(expand_ref.at[pl.ds(middle, middle), :], high_out, 4, sem, moved + 6)
-    later_copies += pieces(reduce_ref, reduce_out, 4, sem, moved + 10)
-    for copy in copies + later_copies:
+    for copy in copies:
         copy.start()
     rows = heads * length
     scale = HEAD_DIM ** (-0.5) * LOG2E
     later = lax.broadcasted_iota(jnp.int32, (rows, length), 1) > (
         lax.broadcasted_iota(jnp.int32, (rows, length), 0) % length
     )
-    span = 4 * length
+    span = 8 * length
     chunks = [
         (ref, start) for ref in (near_ref, far_ref) for start in range(0, ref.shape[0], span)
     ]
+    one = (lax.broadcasted_iota(jnp.int32, (rows, HEAD_DIM), 1) == 0).astype(BF16)
+    for i in range(len(chunks)):
+        for j in range(span // length):
+            hidden = jnp.where(info_ref[1 + i * (span // length) + j] > 0, 0.0, -1e30)
+            bias_ref[i, j * length : (j + 1) * length, :] = jnp.full(
+                (length, HEAD_DIM), hidden, F32
+            ).astype(BF16)
     groups = out_ref.shape[0]
     keep = length // groups
     stacked = []
@@ -149,14 +143,14 @@
             score = jnp.where(later, -1e30, contract(query, own_ref[:, keys], 1, 1))
             score_ref[:, :length] = score
             peak = score
+            marked = jnp.concatenate([query, one], axis=1)
             for i, (ref, start) in enumerate(chunks):
-                score = contract(query, ref[start : start + span, keys], 1, 1)
+                key = jnp.concatenate([ref[start : start + span, keys], bias_ref[i]], axis=1)
+                score = contract(marked, key, 1, 1)
+                at = length + i * span
+                score_ref[:, at : at + span] = score
                 for j in range(0, span, length):
-                    earlier = info_ref[1 + (i * span + j) // length] > 0
-                    part = jnp.where(earlier, score[:, j : j + length], -1e30)
-                    at = length + i * span + j
-                    score_ref[:, at : at + length] = part
-                    peak = jnp.maximum(peak, part)
+                    peak = jnp.maximum(peak, score[:, j : j + length])
             peak = jnp.max(peak, axis=1, keepdims=True)
             weight = jnp.exp2((score_ref[:, :length] - peak) * scale)
             mass = weight
@@ -189,8 +183,6 @@
             out_ref[:, p * keep : (p + 1) * keep, n : n + step] = part[
                 p * length : (p + 1) * length
             ].reshape(groups, keep, step)
-    for copy in later_copies:
-        copy.wait()
 
 
 def prepare_kernel(routing_ref, gate_ref, place_ref, mix_ref):
@@ -276,7 +268,7 @@
         ).astype(BF16)
 
 
-def expert_kernel(x_ref, low_ref, high_ref, w2_ref, out_ref, rows_ref, gated_ref):
+def expert_kernel(x_ref, w1_ref, w2_ref, out_ref, rows_ref, gated_ref):
     slots = rows_ref.shape[0]
     group = 32
     size = group * PARTS
@@ -293,12 +285,10 @@
                 c * group : (c + 1) * group, :
             ]
     for c in range(PARTS):
-        half_ref = low_ref if c < PARTS // 2 else high_ref
-        at = c * PART % half_ref.shape[0]
         for n in range(0, 2 * EW, PART):
             part = jnp.dot(
                 rows_ref[:, c * PART : (c + 1) * PART],
-                half_ref[at : at + PART, n : n + PART],
+                w1_ref[c * PART : (c + 1) * PART, n : n + PART],
                 preferred_element_type=F32,
             )
             if c == 0:
@@ -391,7 +381,7 @@
         out_shape=pltpu.VMEM((local + length * pairs * local // half, half), BF16),
         in_specs=[in_smem, pl.BlockSpec(memory_space=pltpu.HBM), anywhere],
         out_specs=in_vmem,
-        scratch_shapes=[pltpu.SemaphoreType.DMA((1 + half // (pairs * local),))],
+        scratch_shapes=[pltpu.SemaphoreType.DMA((8 + half // (pairs * local),))],
         compiler_params=pltpu.CompilerParams(vmem_limit_bytes=4 * MIB),
         cost_estimate=pl.CostEstimate(flops=0, bytes_accessed=5 * MIB, transcendentals=0),
     )(((1 - side) * half).astype(jnp.int32)[None], hbm_weight, query)
@@ -430,24 +420,20 @@
         (info, place, mix, token_rows, gain)
     )
     in_hbm = pl.BlockSpec(memory_space=pltpu.HBM)
-    projected, low, high, reduce = pl.pallas_call(
+    projected = pl.pallas_call(
         functools.partial(attend_kernel, pairs=pairs, heads=heads),
-        out_shape=(
-            jax.ShapeDtypeStruct((expert_size, rows, half), BF16),
-            pltpu.VMEM((D // 2, 2 * EW), BF16),
-            pltpu.VMEM((D // 2, 2 * EW), BF16),
-            pltpu.VMEM((EW, D), BF16),
-        ),
-        in_specs=[in_smem] + [in_vmem] * 4 + [in_hbm, anywhere, in_hbm, in_hbm],
-        out_specs=(in_vmem,) * 4,
+        out_shape=jax.ShapeDtypeStruct((expert_size, rows, half), BF16),
+        in_specs=[in_smem] + [in_vmem] * 4 + [in_hbm] * 2,
+        out_specs=in_vmem,
         scratch_shapes=[
             pltpu.VMEM((heads * length, (context_size + 1) * length), F32),
+            pltpu.VMEM((2, blocks * length, HEAD_DIM), BF16),
             pltpu.VMEM((local, half), BF16),
             pltpu.VMEM((local, half), BF16),
             pltpu.VMEM((length, pairs * local), BF16),
             pltpu.SemaphoreType.DMA((16,)),
         ],
-        compiler_params=pltpu.CompilerParams(vmem_limit_bytes=16 * MIB),
+        compiler_params=pltpu.CompilerParams(vmem_limit_bytes=22 * MIB),
         cost_estimate=pl.CostEstimate(
             flops=3 * 10**9, bytes_accessed=9 * MIB, transcendentals=4 * 10**6
         ),
@@ -455,14 +441,15 @@
         info,
         query,
         own,
-        near.reshape(blocks * length, -1),
-        far.reshape(blocks * length, -1),
+        pltpu.with_memory_space_constraint(near.reshape(blocks * length, -1), pltpu.VMEM),
+        pltpu.with_memory_space_constraint(far.reshape(blocks * length, -1), pltpu.VMEM),
         hbm_weight,
-        from_side,
-        pltpu.with_memory_space_constraint(expand_weight[0], pltpu.HBM),
-        pltpu.with_memory_space_constraint(reduce_weight[0], pltpu.HBM),
-    )
-
+        pltpu.with_memory_space_constraint(from_side, pltpu.HBM),
+    )
+
+    projected, expand, reduce = lax.optimization_barrier(
+        (projected, expand_weight[0], reduce_weight[0])
+    )
     received = lax.all_to_all(projected, "exp", 0, 0, tiled=True)
 
     outgoing, stream = pl.pallas_call(
@@ -485,7 +472,7 @@
     results = pl.pallas_call(
         expert_kernel,
         out_shape=jax.ShapeDtypeStruct((slots * PARTS, PART), BF16),
-        in_specs=[in_vmem] * 4,
+        in_specs=[in_vmem] * 3,
         out_specs=in_vmem,
         scratch_shapes=[pltpu.VMEM((slots, D), BF16), pltpu.VMEM((slots, 2 * EW), F32)],
         compiler_params=pltpu.CompilerParams(vmem_limit_bytes=10 * MIB),
@@ -494,8 +481,7 @@
         ),
     )(
         arrived,
-        pltpu.with_memory_space_constraint(low, pltpu.VMEM),
-        pltpu.with_memory_space_constraint(high, pltpu.VMEM),
+        pltpu.with_memory_space_constraint(expand, pltpu.VMEM),
         pltpu.with_memory_space_constraint(reduce, pltpu.VMEM),
     )
     returned = lax.all_to_all(

time: 174 us -> 171 us (0.983)
  Pallas kernels: 28.1 us -> 25.4 us
where the time goes in v3:
time: 171 us
  blocking collectives  139 us (81%)
  Pallas kernels  25.4 us (15%)
  starting transfers between devices  4.13 us (2%)
  local copies, waits for them, and re-layouts  2.52 us (1%)
    all_to_all x1, blocking collectives, shards(): lax.all_to_all(outgoing.reshape(exchanged), ('ctx', 'exp'), 0, 0, tiled=T...  50.3 us
    all_to_all x1, blocking collectives, shards(): lax.all_to_all(results.reshape(exchanged), ('ctx', 'exp'), 0, 0, tiled=True)  45.9 us
    all_to_all x1, blocking collectives, shards(): lax.all_to_all(jnp.broadcast_to(own[None], (blocks,) + own.shape), 'ctx',...  25 us
    all_to_all x1, blocking collectives, shards(): received = lax.all_to_all(projected, 'exp', 0, 0, tiled=True)  17.5 us
    pallas_call x1, Pallas kernels, shards(): pl.pallas_call(functools.partial(attend_kernel, pairs=pairs, heads=heads)...  9.82 us
    pallas_call x1, Pallas kernels, shards(): pl.pallas_call(expert_kernel, out_shape=jax.ShapeDtypeStruct((slots * PAR...  9.21 us
  transfers between devices with their start and end apart: 2, of which 0 were waited for; matrix products, arithmetic and copies ran while one was open for 0% of the time, Pallas kernels for 1%

profile of v3, /device:TPU:1, one launch (start us, length us, event | category | flops | bytes accessed | tf_op | source)
XLA Modules:
  0.0 171.2 jit_solution(7839589487654152901)
XLA Ops:
  0.0 1.0 copy.15
  1.0 0.0 copy-start.1
  1.0 0.0 copy-start.2
  1.0 1.6 shard_map.101
  2.7 0.0 copy-start.3
  2.7 0.0 copy-start.4
  2.7 0.0 copy-start.5
  2.7 0.0 copy-start
  2.7 3.4 %collective-permute-start.1 = (bf16[576,2048]{1,0:T(8,128)(2,1)S(1)}, bf16[576,2048]{1,0:T(8,128)(2,1)}, u32[]{:S(2)}, u32[]{:S(2)}) collective-permute-start(bf16[576,2048]{1,0:T(8,128)(2,1)S(1)} %shard_map.101), channel_id=1, source_target_pairs={{0,1},{1,0},{2,3},{3,2},{4,5},{5,4},{6,7},{7,6},{8,11},{9,10},{10,... | collective-permute-start | bytes 7077896 | tf_op jit(solution)/shard_map/ppermute | solution.py:388
  6.1 0.0 copy-done.1
  6.1 0.0 copy-done.2
  6.1 0.1 constant_dynamic-slice_fusion
  6.2 0.1 pad_maximum_fusion
  6.4 0.1 broadcast_in_dim.16
  6.5 25.0 %all_to_all.20 = bf16[8,128,512]{2,1,0:T(8,128)(2,1)} all-to-all(bf16[8,128,512]{2,1,0:T(8,128)(2,1)S(1)} %broadcast_in_dim.16), channel_id=1, replica_groups={{0,16,32,48,64,80,96,112},{8,24,40,56,72,88,104,120},{1,17,33,49,65,81,..., dimensions={0} | all-to-all | bytes 2097152 | tf_op jit(solution)/shard_map/all_to_all | solution.py:390
  31.4 0.7 collective-permute-start
  32.2 0.0 copy-done.3
  32.2 0.0 copy-done.4
  32.2 0.1 copy.11
  32.3 0.0 copy-done.5
  32.3 0.1 copy.12
  32.4 0.0 copy-done
  32.4 0.2 copy.13
  32.5 0.0 slice-start.3
  32.5 2.5 %shard_map.100 = (bf16[3072,256]{1,0:T(8,128)(2,1)S(1)}, bf16[256,3072]{1,0:T(8,128)(2,1)S(1)}) custom-call(s32[32,8]{1,0:T(8,128)S(1)} %bitcast.34, f32[32,8]{1,0:T(8,128)S(1)} %bitcast.35), custom_call_target="tpu_custom_call" | custom-call | flops 1000000000 | bytes 3145728 | tf_op jit(solution)/shard_map/pallas_call | solution.py:407
  35.1 0.1 compare_convert_fusion
  35.1 0.1 pad_add_fusion.info_ref
  35.2 0.0 collective-permute-done
  35.2 0.0 collective-permute-done.1.side_ref
  35.2 0.0 slice-start
  35.2 0.0 slice-start.1
  35.2 0.0 slice-start.4
  35.3 9.8 %shard_map.102 = bf16[8,32,2048]{2,1,0:T(8,128)(2,1)S(1)} custom-call(s32[17]{0:T(128)S(1)} %pad_add_fusion.info_ref, bf16[128,1024]{1,0:T(8,128)(2,1)S(1)} %bitcast.29, bf16[128,512]{1,0:T(8,128)(2,1)S(1)} %bitcast.32, bf16[1024,512]{1,0:T(8,128)(2,1)} %bitcast.7.near_ref, bf16[1024,512]{1,0:T(8,128)(2,1)} %bitcast.8.far_ref, bf16[512,4096]{1,0:T(8,128)(2,1)} %weight_ref.3, ...), custom_call_target="tpu_custom_call" | custom-call | flops 3000000000 | bytes 9437184 | tf_op jit(solution)/shard_map/pallas_call | solution.py:423
  45.1 17.5 %all_to_all.21.part_ref = bf16[8,32,2048]{2,1,0:T(8,128)(2,1)S(1)} all-to-all(bf16[8,32,2048]{2,1,0:T(8,128)(2,1)S(1)} %shard_map.102), channel_id=1, replica_groups=mesh['ctx'=16,'exp'=8] {'exp'}, dimensions={0} | all-to-all | bytes 2097152 | tf_op jit(solution)/shard_map/all_to_all | solution.py:453
  62.6 0.0 slice-start.2
  62.6 1.3 shard_map.103
  63.8 50.3 %all_to_all.22 = bf16[128,24,512]{2,1,0:T(8,128)(2,1)S(1)} all-to-all(bf16[128,24,512]{2,1,0:T(8,128)(2,1)S(1)} %bitcast.25), channel_id=1, replica_groups=mesh['ctx'=16,'exp'=8] {'ctx','exp'}, dimensions={0} | all-to-all | bytes 6291456 | tf_op jit(solution)/shard_map/all_to_all | solution.py:469
  114.1 0.0 slice-done.3
  114.1 0.0 slice-done
  114.1 0.0 slice-done.1
  114.1 0.0 slice-done.4
  114.1 0.0 slice-done.2
  114.2 9.2 %shard_map.104 = bf16[3072,512]{1,0:T(8,128)(2,1)S(1)} custom-call(bf16[3072,512]{1,0:T(8,128)(2,1)S(1)} %bitcast.26, bf16[4096,1536]{1,0:T(8,128)(2,1)S(1)} %bitcast.38, bf16[768,4096]{1,0:T(8,128)(2,1)S(1)} %bitcast.41), custom_call_target="tpu_custom_call" | custom-call | flops 8000000000 | bytes 6291456 | tf_op jit(solution)/shard_map/pallas_call | solution.py:472
  123.4 45.9 %all_to_all.23 = bf16[128,24,512]{2,1,0:T(8,128)(2,1)S(1)} all-to-all(bf16[128,24,512]{2,1,0:T(8,128)(2,1)S(1)} %bitcast.27), channel_id=1, replica_groups=mesh['ctx'=16,'exp'=8] {'ctx','exp'}, dimensions={0} | all-to-all | bytes 6291456 | tf_op jit(solution)/shard_map/all_to_all | solution.py:487
  169.2 1.0 shard_map.105
  170.2 1.0 copy.18
  (5 shorter events, 0.0 us)
Async XLA Ops:
  1.0 5.1 %copy-start.1 = (bf16[128,2,256]{2,1,0:T(2,128)(2,1)S(1)}, bf16[128,2,256]{2,1,0:T(2,128)(2,1)}, u32[]{:S(2)}) copy-start(bf16[128,2,256]{2,1,0:T(2,128)(2,1)} %param.13) | copy-start | bytes 393220
  1.0 5.1 %copy-start.2 = (bf16[128,2,256]{2,1,0:T(2,128)(2,1)S(1)}, bf16[128,2,256]{2,1,0:T(2,128)(2,1)}, u32[]{:S(2)}) copy-start(bf16[128,2,256]{2,1,0:T(2,128)(2,1)} %param.12) | copy-start | bytes 393220
  2.7 29.5 %copy-start.3 = (bf16[4096]{0:T(1024)(128)(2,1)S(1)}, bf16[4096]{0:T(1024)(128)(2,1)}, u32[]{:S(2)}) copy-start(bf16[4096]{0:T(1024)(128)(2,1)} %param.15) | copy-start | bytes 24580
  2.7 29.5 %copy-start.4 = (s32[16,2,8]{0,2,1:T(8,128)S(1)}, s32[16,2,8]{0,2,1:T(8,128)}, u32[]{:S(2)}) copy-start(s32[16,2,8]{0,2,1:T(8,128)} %param.16) | copy-start | bytes 3076
  2.7 29.6 %copy-start.5 = (f32[16,2,8]{0,2,1:T(8,128)S(1)}, f32[16,2,8]{0,2,1:T(8,128)}, u32[]{:S(2)}) copy-start(f32[16,2,8]{0,2,1:T(8,128)} %param.17) | copy-start | bytes 3076
  2.7 29.7 %copy-start = (bf16[16,2,4096]{2,1,0:T(2,128)(2,1)S(1)}, bf16[16,2,4096]{2,1,0:T(2,128)(2,1)}, u32[]{:S(2)}) copy-start(bf16[16,2,4096]{2,1,0:T(2,128)(2,1)} %param.10) | copy-start | bytes 786436
  2.7 32.5 %collective-permute-start.1 = (bf16[576,2048]{1,0:T(8,128)(2,1)S(1)}, bf16[576,2048]{1,0:T(8,128)(2,1)}, u32[]{:S(2)}, u32[]{:S(2)}) collective-permute-start(bf16[576,2048]{1,0:T(8,128)(2,1)S(1)} %shard_map.101), channel_id=1, source_target_pairs={{0,1},{1,0},{2,3},{3,2},{4,5},{5,4},{6,7},{7,6},{8,11},{9,10},{10,... | collective-permute-start | bytes 7077896 | tf_op jit(solution)/shard_map/ppermute | solution.py:388
  31.4 3.8 %collective-permute-start = (bf16[8,128,512]{2,1,0:T(8,128)(2,1)}, bf16[8,128,512]{2,1,0:T(8,128)(2,1)}, u32[]{:S(2)}, u32[]{:S(2)}) collective-permute-start(bf16[8,128,512]{2,1,0:T(8,128)(2,1)} %all_to_all.20), channel_id=1, source_target_pairs={{0,8},{8,0},{16,24},{24,16},{32,40},{40,32},{48,56},{56,48},{64,72... | collective-permute-start | bytes 3145736 | tf_op jit(solution)/shard_map/ppermute | solution.py:398
  32.5 81.6 %slice-start.3 = ((s8[6291456]{0:T(1024)(128)(4,1)}), s8[4194304]{0:T(1024)(128)(4,1)S(1)}, s32[]{:S(2)}) async-start(s8[6291456]{0:T(1024)(128)(4,1)} %bitcast.39), calls=%async_computation.7 | async-start | bytes 8388608
  35.2 78.9 %slice-start = ((s8[12582912]{0:T(1024)(128)(4,1)}), s8[4194304]{0:T(1024)(128)(4,1)S(1)}, s32[]{:S(2)}) async-start(s8[12582912]{0:T(1024)(128)(4,1)} %bitcast.36), calls=%async_computation.4 | async-start | bytes 8388608
  35.2 78.9 %slice-start.1 = ((s8[12582912]{0:T(1024)(128)(4,1)}), s8[4194304]{0:T(1024)(128)(4,1)S(1)}, s32[]{:S(2)}) async-start(s8[12582912]{0:T(1024)(128)(4,1)} %bitcast.36), calls=%async_computation.5 | async-start | bytes 8388608
  35.2 78.9 %slice-start.4 = ((s8[6291456]{0:T(1024)(128)(4,1)}), s8[2097152]{0:T(1024)(128)(4,1)S(1)}, s32[]{:S(2)}) async-start(s8[6291456]{0:T(1024)(128)(4,1)} %bitcast.39), calls=%async_computation.8 | async-start | bytes 4194304
  62.6 51.6 %slice-start.2 = ((s8[12582912]{0:T(1024)(128)(4,1)}), s8[4194304]{0:T(1024)(128)(4,1)S(1)}, s32[]{:S(2)}) async-start(s8[12582912]{0:T(1024)(128)(4,1)} %bitcast.36), calls=%async_computation.6 | async-start | bytes 8388608

commit v4 on v3

--- a/solution.py
+++ b/solution.py
@@ -16,6 +16,8 @@
 CAP = 3
 PARTS = 8
 PART = D // PARTS
+ALONE = 256
+TILE = 16
 LOG2E = 1.4426950408889634
 F32 = jnp.float32
 BF16 = jnp.bfloat16
@@ -40,24 +42,45 @@
     ]
 
 
-def pack_kernel(info_ref, weight_ref, query_ref, out_ref, sem):
+def pack_kernel(info_ref, weight_ref, query_ref, out_ref, flat_ref, buf_ref, query_buf, sem):
     depth = weight_ref.shape[0]
     width = out_ref.shape[1]
     extra = out_ref.shape[0] - depth
-    cols = query_ref.shape[1]
-    columns = weight_ref.at[:, pl.ds(pl.multiple_of(info_ref[0], width), width)]
-    copies = pieces(columns, out_ref.at[pl.ds(0, depth), :], 8, sem, 0)
-    for i in range(width // cols):
-        copies.append(
-            pltpu.make_async_copy(
-                query_ref.at[pl.ds(i * extra, extra), :],
-                out_ref.at[pl.ds(depth, extra), pl.ds(i * cols, cols)],
-                sem.at[8 + i],
-            )
+    length, pairs, local = query_ref.shape
+    count = 8
+    columns = weight_ref.at[:, pl.ds(pl.multiple_of(info_ref[0], PART), width)]
+    query_copy = pltpu.make_async_copy(query_ref, query_buf, sem.at[0])
+    query_copy.start()
+    inward = pieces(columns, buf_ref.at[pl.ds(0, depth), :], count, sem, 1)
+    outward = pieces(
+        buf_ref.at[pl.ds(0, depth), :], out_ref.at[pl.ds(0, depth), :], count, sem, 1 + count
+    )
+    tail = pl.ds(depth, extra)
+    outward.append(
+        pltpu.make_async_copy(
+            buf_ref.at[tail, :], out_ref.at[tail, :], sem.at[1 + 2 * count]
         )
-    for copy in copies:
+    )
+    for copy in inward:
         copy.start()
-    for copy in copies:
+    query_copy.wait()
+    lanes = width // HEAD_DIM
+    for p in range(pairs):
+        query = query_buf[:, p, :]
+        flat_ref[:, p * local : (p + 1) * local] = query
+        for h in range(local // HEAD_DIM):
+            for r in range(length // TILE):
+                slot = (p * local // HEAD_DIM + h) * (length // TILE) + r
+                row = depth + slot // lanes * TILE
+                at = slot % lanes * HEAD_DIM
+                buf_ref[row : row + TILE, at : at + HEAD_DIM] = query[
+                    r * TILE : (r + 1) * TILE, h * HEAD_DIM : (h + 1) * HEAD_DIM
+                ]
+    outward[count].start()
+    for i in range(count):
+        inward[i].wait()
+        outward[i].start()
+    for copy in outward:
         copy.wait()
 
 
@@ -81,28 +104,27 @@
     heads,
 ):
     length = own_ref.shape[0]
-    depth, half = w0_ref.shape
-    extra = side_ref.shape[0] - depth
-    cols = q1_ref.shape[1]
+    depth = w0_ref.shape[0]
+    shared = w1_ref.shape[1]
+    half = shared + ALONE
     copies = [
         pltpu.make_async_copy(
-            side_ref.at[pl.ds(depth, extra), pl.ds(i * cols, cols)],
-            q1_ref.at[pl.ds(i * extra, extra), :],
-            sem.at[i],
-        )
-        for i in range(half // cols)
-    ]
-    moved = len(copies)
-    copies.append(
+            side_ref.at[pl.ds(depth, q1_ref.shape[0]), :], q1_ref, sem.at[0]
+        ),
         pltpu.make_async_copy(
             weight_ref.at[:, pl.ds(pl.multiple_of(info_ref[0], half), half)],
-            w0_ref,
-            sem.at[moved],
-        )
-    )
-    copies.append(
-        pltpu.make_async_copy(side_ref.at[pl.ds(0, depth), :], w1_ref, sem.at[moved + 1])
-    )
+            w0_ref.at[:, pl.ds(0, half)],
+            sem.at[1],
+        ),
+        pltpu.make_async_copy(
+            weight_ref.at[:, pl.ds(pl.multiple_of(half - info_ref[0] + shared, ALONE), ALONE)],
+            w0_ref.at[:, pl.ds(half, ALONE)],
+            sem.at[2],
+        ),
+        pltpu.make_async_copy(side_ref.at[pl.ds(0, depth), :], w1_ref, sem.at[3]),
+    ]
+    moved = 1
+    lanes = shared // HEAD_DIM
     for copy in copies:
         copy.start()
     rows = heads * length
@@ -132,14 +154,15 @@
         for p in range(pairs):
             keys = slice(p * 2 * HEAD_DIM, (p * 2 + 1) * HEAD_DIM)
             values = slice((p * 2 + 1) * HEAD_DIM, (p * 2 + 2) * HEAD_DIM)
-            first = p * heads * HEAD_DIM
-            query = jnp.concatenate(
-                [
-                    q_ref[:, first + h * HEAD_DIM : first + (h + 1) * HEAD_DIM]
-                    for h in range(heads)
-                ],
-                axis=0,
-            )
+            blocks = []
+            for head in range(p * heads, (p + 1) * heads):
+                if q_ref is q0_ref:
+                    blocks.append(q_ref[:, head * HEAD_DIM : (head + 1) * HEAD_DIM])
+                    continue
+                for slot in range(head * (length // TILE), (head + 1) * (length // TILE)):
+                    row, at = slot // lanes * TILE, slot % lanes * HEAD_DIM
+                    blocks.append(q_ref[row : row + TILE, at : at + HEAD_DIM])
+            query = jnp.concatenate(blocks, axis=0)
             score = jnp.where(later, -1e30, contract(query, own_ref[:, keys], 1, 1))
             score_ref[:, :length] = score
             peak = score
@@ -174,10 +197,13 @@
         stacked.append(jnp.concatenate(attended, axis=0))
     for copy in copies[moved:]:
         copy.wait()
-    step = half // 4
-    for n in range(0, half, step):
+    step = ALONE
+    for n in range(0, half + ALONE, step):
         part = jnp.dot(stacked[0], w0_ref[:, n : n + step], preferred_element_type=F32)
-        part = part + jnp.dot(stacked[1], w1_ref[:, n : n + step], preferred_element_type=F32)
+        if n < shared:
+            part = part + jnp.dot(
+                stacked[1], w1_ref[:, n : n + step], preferred_element_type=F32
+            )
         part = part.astype(BF16)
         for p in range(pairs):
             out_ref[:, p * keep : (p + 1) * keep, n : n + step] = part[
@@ -245,6 +271,14 @@
         total = total + sum(
             part_ref[s, :, at].astype(F32) for s in range(c // half, sources, 2)
         )
+        if c % half == half - 1:
+            alone = sum(
+                part_ref[s, :, D // 2 :].astype(F32)
+                for s in range(1 - c // half, sources, 2)
+            )
+            total = jnp.concatenate(
+                [total[:, : PART - ALONE], total[:, PART - ALONE :] + alone], axis=1
+            )
         stream = total.astype(BF16)
         stream_ref[c * rows : (c + 1) * rows, :] = stream
         wide = stream.astype(F32)
@@ -372,19 +406,29 @@
     ]
     hbm_weight = pltpu.with_memory_space_constraint(output_weight, pltpu.HBM)
     half = D // 2
-    query = queries.reshape(length, pairs * local)
     in_vmem = pl.BlockSpec(memory_space=pltpu.VMEM)
     anywhere = pl.BlockSpec(memory_space=pl.ANY)
     in_smem = pl.BlockSpec(memory_space=pltpu.SMEM)
-    sent = pl.pallas_call(
+    in_hbm = pl.BlockSpec(memory_space=pltpu.HBM)
+    shared = half - ALONE
+    query_rows = -(-length * pairs * local // (shared * TILE)) * TILE
+    packed_rows = local + query_rows
+    sent, query = pl.pallas_call(
         pack_kernel,
-        out_shape=pltpu.VMEM((local + length * pairs * local // half, half), BF16),
-        in_specs=[in_smem, pl.BlockSpec(memory_space=pltpu.HBM), anywhere],
-        out_specs=in_vmem,
-        scratch_shapes=[pltpu.SemaphoreType.DMA((8 + half // (pairs * local),))],
-        compiler_params=pltpu.CompilerParams(vmem_limit_bytes=4 * MIB),
+        out_shape=(
+            jax.ShapeDtypeStruct((packed_rows, shared), BF16),
+            jax.ShapeDtypeStruct((length, pairs * local), BF16),
+        ),
+        in_specs=[in_smem, in_hbm, in_hbm],
+        out_specs=(in_hbm, in_vmem),
+        scratch_shapes=[
+            pltpu.VMEM((packed_rows, shared), BF16),
+            pltpu.VMEM(queries.shape, BF16),
+            pltpu.SemaphoreType.DMA((18,)),
+        ],
+        compiler_params=pltpu.CompilerParams(vmem_limit_bytes=8 * MIB),
         cost_estimate=pl.CostEstimate(flops=0, bytes_accessed=5 * MIB, transcendentals=0),
-    )(((1 - side) * half).astype(jnp.int32)[None], hbm_weight, query)
+    )(((1 - side) * half).astype(jnp.int32)[None], hbm_weight, pltpu.with_memory_space_constraint(queries, pltpu.HBM))
     from_side = lax.ppermute(sent, ("ctx", "exp"), swap_side)
     same = [[c for c in range(k, context_size, 2)] for k in range(2)]
     near = lax.all_to_all(
@@ -419,19 +463,18 @@
     info, place, mix, token_rows, gain = lax.optimization_barrier(
         (info, place, mix, token_rows, gain)
     )
-    in_hbm = pl.BlockSpec(memory_space=pltpu.HBM)
     projected = pl.pallas_call(
         functools.partial(attend_kernel, pairs=pairs, heads=heads),
-        out_shape=jax.ShapeDtypeStruct((expert_size, rows, half), BF16),
+        out_shape=jax.ShapeDtypeStruct((expert_size, rows, half + ALONE), BF16),
         in_specs=[in_smem] + [in_vmem] * 4 + [in_hbm] * 2,
         out_specs=in_vmem,
         scratch_shapes=[
             pltpu.VMEM((heads * length, (context_size + 1) * length), F32),
             pltpu.VMEM((2, blocks * length, HEAD_DIM), BF16),
-            pltpu.VMEM((local, half), BF16),
-            pltpu.VMEM((local, half), BF16),
-            pltpu.VMEM((length, pairs * local), BF16),
-            pltpu.SemaphoreType.DMA((16,)),
+            pltpu.VMEM((local, half + ALONE), BF16),
+            pltpu.VMEM((local, shared), BF16),
+            pltpu.VMEM((query_rows, shared), BF16),
+            pltpu.SemaphoreType.DMA((4,)),
         ],
         compiler_params=pltpu.CompilerParams(vmem_limit_bytes=22 * MIB),
         cost_estimate=pl.CostEstimate(

time: 171 us -> 170 us (level)
    all_to_all x1, blocking collectives: 50.3 us -> 47.7 us  [shards(): lax.all_to_all(outgoing.reshape(exchanged), ('ctx', 'exp'), 0, 0, tiled=T...]
    all_to_all x1, blocking collectives: 17.5 us -> 19.3 us  [shards(): received = lax.all_to_all(projected, 'exp', 0, 0, tiled=True)]
where the time goes in v4:
time: 170 us
  blocking collectives  138 us (81%)
  Pallas kernels  25.7 us (15%)
  starting transfers between devices  4.13 us (2%)
    all_to_all x1, blocking collectives, shards(): lax.all_to_all(outgoing.reshape(exchanged), ('ctx', 'exp'), 0, 0, tiled=T...  47.7 us
    all_to_all x1, blocking collectives, shards(): lax.all_to_all(results.reshape(exchanged), ('ctx', 'exp'), 0, 0, tiled=True)  45.9 us
    all_to_all x1, blocking collectives, shards(): lax.all_to_all(jnp.broadcast_to(own[None], (blocks,) + own.shape), 'ctx',...  24.9 us
    all_to_all x1, blocking collectives, shards(): received = lax.all_to_all(projected, 'exp', 0, 0, tiled=True)  19.3 us
    pallas_call x1, Pallas kernels, shards(): pl.pallas_call(expert_kernel, out_shape=jax.ShapeDtypeStruct((slots * PAR...  9.21 us
    pallas_call x1, Pallas kernels, shards(): pl.pallas_call(functools.partial(attend_kernel, pairs=pairs, heads=heads)...  8.55 us
  transfers between devices with their start and end apart: 2, of which 0 were waited for; matrix products, arithmetic and copies ran while one was open for 0% of the time, Pallas kernels for 1%

profile of v4, /device:TPU:1, one launch (start us, length us, event | category | flops | bytes accessed | tf_op | source)
XLA Modules:
  0.0 169.7 jit_solution(14652460477108127687)
XLA Ops:
  0.0 0.0 copy-start.1
  0.0 0.0 copy-start.2
  0.0 3.2 %shard_map.101 = (bf16[592,1792]{1,0:T(8,128)(2,1)}, bf16[128,1024]{1,0:T(8,128)(2,1)S(1)}) custom-call(s32[1]{0:T(128)} %bitcast.7.info_ref, bf16[512,4096]{1,0:T(8,128)(2,1)} %weight_ref.3, bf16[128,2,512]{2,1,0:T(2,128)(2,1)} %query_ref.1), custom_call_target="tpu_custom_call" | custom-call | bytes 5242880 | tf_op jit(solution)/shard_map/pallas_call | solution.py:416
  3.2 0.0 copy-start.3
  3.2 0.0 copy-start.4
  3.2 0.0 copy-start.5
  3.2 0.0 copy-start
  3.3 3.4 %collective-permute-start.1 = (bf16[592,1792]{1,0:T(8,128)(2,1)}, bf16[592,1792]{1,0:T(8,128)(2,1)}, u32[]{:S(2)}, u32[]{:S(2)}) collective-permute-start(bf16[592,1792]{1,0:T(8,128)(2,1)} %get-tuple-element.23), channel_id=1, source_target_pairs={{0,1},{1,0},{2,3},{3,2},{4,5},{5,4},{6,7},{7,6},{8,11},{9,10},{10,... | collective-permute-start | bytes 6365192 | tf_op jit(solution)/shard_map/ppermute | solution.py:432
  6.6 0.0 copy-done.1
  6.7 0.0 copy-done.2
  6.7 0.1 constant_dynamic-slice_fusion
  6.8 0.1 pad_maximum_fusion
  6.9 0.1 broadcast_in_dim.17
  7.0 24.9 %all_to_all.20 = bf16[8,128,512]{2,1,0:T(8,128)(2,1)S(1)} all-to-all(bf16[8,128,512]{2,1,0:T(8,128)(2,1)S(1)} %broadcast_in_dim.17), channel_id=1, replica_groups={{0,16,32,48,64,80,96,112},{8,24,40,56,72,88,104,120},{1,17,33,49,65,81,..., dimensions={0} | all-to-all | bytes 2097152 | tf_op jit(solution)/shard_map/all_to_all | solution.py:434
  31.9 0.7 collective-permute-start
  32.6 0.0 copy-done.3
  32.6 0.0 copy-done.4
  32.7 0.1 copy.11
  32.7 0.0 copy-done.5
  32.7 0.1 copy.12
  32.8 0.0 copy-done
  32.8 0.2 copy.13
  33.0 0.0 slice-start.3
  33.0 2.5 %shard_map.100 = (bf16[3072,256]{1,0:T(8,128)(2,1)S(1)}, bf16[256,3072]{1,0:T(8,128)(2,1)S(1)}) custom-call(s32[32,8]{1,0:T(8,128)S(1)} %bitcast.31, f32[32,8]{1,0:T(8,128)S(1)} %bitcast.32), custom_call_target="tpu_custom_call" | custom-call | flops 1000000000 | bytes 3145728 | tf_op jit(solution)/shard_map/pallas_call | solution.py:451
  35.5 0.1 compare_convert_fusion
  35.6 0.1 pad_add_fusion.info_ref
  35.7 0.0 collective-permute-done
  35.7 0.0 collective-permute-done.1.side_ref
  35.7 0.0 slice-start
  35.7 0.0 slice-start.1
  35.7 0.0 slice-start.4
  35.7 8.6 %shard_map.102 = bf16[8,32,2304]{2,1,0:T(8,128)(2,1)S(1)} custom-call(s32[17]{0:T(128)S(1)} %pad_add_fusion.info_ref, bf16[128,1024]{1,0:T(8,128)(2,1)S(1)} %get-tuple-element.22.q0_ref, bf16[128,512]{1,0:T(8,128)(2,1)S(1)} %bitcast.29, bf16[1024,512]{1,0:T(8,128)(2,1)S(1)} %bitcast.27, bf16[1024,512]{1,0:T(8,128)(2,1)S(1)} %bitcast.39, ...), custom_call_target="tpu_custom_call" | custom-call | flops 3000000000 | bytes 9437184 | tf_op jit(solution)/shard_map/pallas_call | solution.py:466
  44.3 19.3 %all_to_all.21.part_ref = bf16[8,32,2304]{2,1,0:T(8,128)(2,1)S(1)} all-to-all(bf16[8,32,2304]{2,1,0:T(8,128)(2,1)S(1)} %shard_map.102), channel_id=1, replica_groups=mesh['ctx'=16,'exp'=8] {'exp'}, dimensions={0} | all-to-all | bytes 2359296 | tf_op jit(solution)/shard_map/all_to_all | solution.py:496
  63.6 0.0 slice-start.2
  63.6 1.3 shard_map.103
  64.9 47.7 %all_to_all.22 = bf16[128,24,512]{2,1,0:T(8,128)(2,1)S(1)} all-to-all(bf16[128,24,512]{2,1,0:T(8,128)(2,1)S(1)} %bitcast.23), channel_id=1, replica_groups=mesh['ctx'=16,'exp'=8] {'ctx','exp'}, dimensions={0} | all-to-all | bytes 6291456 | tf_op jit(solution)/shard_map/all_to_all | solution.py:512
  112.7 0.0 slice-done.3
  112.7 0.0 slice-done
  112.7 0.0 slice-done.1
  112.7 0.0 slice-done.4
  112.7 0.0 slice-done.2
  112.7 9.2 %shard_map.104 = bf16[3072,512]{1,0:T(8,128)(2,1)S(1)} custom-call(bf16[3072,512]{1,0:T(8,128)(2,1)S(1)} %bitcast.24, bf16[4096,1536]{1,0:T(8,128)(2,1)S(1)} %bitcast.35, bf16[768,4096]{1,0:T(8,128)(2,1)S(1)} %bitcast.38), custom_call_target="tpu_custom_call" | custom-call | flops 8000000000 | bytes 6291456 | tf_op jit(solution)/shard_map/pallas_call | solution.py:515
  121.9 45.9 %all_to_all.23 = bf16[128,24,512]{2,1,0:T(8,128)(2,1)S(1)} all-to-all(bf16[128,24,512]{2,1,0:T(8,128)(2,1)S(1)} %bitcast.25), channel_id=1, replica_groups=mesh['ctx'=16,'exp'=8] {'ctx','exp'}, dimensions={0} | all-to-all | bytes 6291456 | tf_op jit(solution)/shard_map/all_to_all | solution.py:530
  167.8 1.0 shard_map.105
  168.8 1.0 copy.17
  (5 shorter events, 0.0 us)
Async XLA Ops:
  0.0 6.7 %copy-start.1 = (bf16[128,2,256]{2,1,0:T(2,128)(2,1)S(1)}, bf16[128,2,256]{2,1,0:T(2,128)(2,1)}, u32[]{:S(2)}) copy-start(bf16[128,2,256]{2,1,0:T(2,128)(2,1)} %param.13) | copy-start | bytes 393220
  0.0 6.7 %copy-start.2 = (bf16[128,2,256]{2,1,0:T(2,128)(2,1)S(1)}, bf16[128,2,256]{2,1,0:T(2,128)(2,1)}, u32[]{:S(2)}) copy-start(bf16[128,2,256]{2,1,0:T(2,128)(2,1)} %param.12) | copy-start | bytes 393220
  3.2 29.4 %copy-start.3 = (bf16[4096]{0:T(1024)(128)(2,1)S(1)}, bf16[4096]{0:T(1024)(128)(2,1)}, u32[]{:S(2)}) copy-start(bf16[4096]{0:T(1024)(128)(2,1)} %param.15) | copy-start | bytes 24580
  3.2 29.4 %copy-start.4 = (s32[16,2,8]{0,2,1:T(8,128)S(1)}, s32[16,2,8]{0,2,1:T(8,128)}, u32[]{:S(2)}) copy-start(s32[16,2,8]{0,2,1:T(8,128)} %param.16) | copy-start | bytes 3076
  3.2 29.5 %copy-start.5 = (f32[16,2,8]{0,2,1:T(8,128)S(1)}, f32[16,2,8]{0,2,1:T(8,128)}, u32[]{:S(2)}) copy-start(f32[16,2,8]{0,2,1:T(8,128)} %param.17) | copy-start | bytes 3076
  3.2 29.6 %copy-start = (bf16[16,2,4096]{2,1,0:T(2,128)(2,1)S(1)}, bf16[16,2,4096]{2,1,0:T(2,128)(2,1)}, u32[]{:S(2)}) copy-start(bf16[16,2,4096]{2,1,0:T(2,128)(2,1)} %param.10) | copy-start | bytes 786436
  3.3 32.4 %collective-permute-start.1 = (bf16[592,1792]{1,0:T(8,128)(2,1)}, bf16[592,1792]{1,0:T(8,128)(2,1)}, u32[]{:S(2)}, u32[]{:S(2)}) collective-permute-start(bf16[592,1792]{1,0:T(8,128)(2,1)} %get-tuple-element.23), channel_id=1, source_target_pairs={{0,1},{1,0},{2,3},{3,2},{4,5},{5,4},{6,7},{7,6},{8,11},{9,10},{10,... | collective-permute-start | bytes 6365192 | tf_op jit(solution)/shard_map/ppermute | solution.py:432
  31.9 3.8 %collective-permute-start = (bf16[8,128,512]{2,1,0:T(8,128)(2,1)S(1)}, bf16[8,128,512]{2,1,0:T(8,128)(2,1)S(1)}, u32[]{:S(2)}, u32[]{:S(2)}) collective-permute-start(bf16[8,128,512]{2,1,0:T(8,128)(2,1)S(1)} %all_to_all.20), channel_id=1, source_target_pairs={{0,8},{8,0},{16,24},{24,16},{32,40},{40,32},{48,56},{56,48},{64,72... | collective-permute-start | bytes 3145736 | tf_op jit(solution)/shard_map/ppermute | solution.py:442
  33.0 79.7 %slice-start.3 = ((s8[6291456]{0:T(1024)(128)(4,1)}), s8[4194304]{0:T(1024)(128)(4,1)S(1)}, s32[]{:S(2)}) async-start(s8[6291456]{0:T(1024)(128)(4,1)} %bitcast.36), calls=%async_computation.7 | async-start | bytes 8388608
  35.7 77.0 %slice-start = ((s8[12582912]{0:T(1024)(128)(4,1)}), s8[4194304]{0:T(1024)(128)(4,1)S(1)}, s32[]{:S(2)}) async-start(s8[12582912]{0:T(1024)(128)(4,1)} %bitcast.33), calls=%async_computation.4 | async-start | bytes 8388608
  35.7 77.0 %slice-start.1 = ((s8[12582912]{0:T(1024)(128)(4,1)}), s8[4194304]{0:T(1024)(128)(4,1)S(1)}, s32[]{:S(2)}) async-start(s8[12582912]{0:T(1024)(128)(4,1)} %bitcast.33), calls=%async_computation.5 | async-start | bytes 8388608
  35.7 77.0 %slice-start.4 = ((s8[6291456]{0:T(1024)(128)(4,1)}), s8[2097152]{0:T(1024)(128)(4,1)S(1)}, s32[]{:S(2)}) async-start(s8[6291456]{0:T(1024)(128)(4,1)} %bitcast.36), calls=%async_computation.8 | async-start | bytes 4194304
  63.6 49.1 %slice-start.2 = ((s8[12582912]{0:T(1024)(128)(4,1)}), s8[4194304]{0:T(1024)(128)(4,1)S(1)}, s32[]{:S(2)}) async-start(s8[12582912]{0:T(1024)(128)(4,1)} %bitcast.33), calls=%async_computation.6 | async-start | bytes 8388608

commit v5 on v4

--- a/solution.py
+++ b/solution.py
@@ -63,6 +63,9 @@
     )
     for copy in inward:
         copy.start()
+    for i in range(count):
+        inward[i].wait()
+        outward[i].start()
     query_copy.wait()
     lanes = width // HEAD_DIM
     for p in range(pairs):
@@ -77,9 +80,6 @@
                     r * TILE : (r + 1) * TILE, h * HEAD_DIM : (h + 1) * HEAD_DIM
                 ]
     outward[count].start()
-    for i in range(count):
-        inward[i].wait()
-        outward[i].start()
     for copy in outward:
         copy.wait()
 
@@ -235,23 +235,19 @@
     wide = contract(rank.astype(BF16), spread, 0, 0).astype(BF16)
     chunk = 768
     for s in range(0, slots, chunk):
-        slot = s + lax.broadcasted_iota(jnp.int32, (chunk, experts), 0)
-        owner = (
-            slot // (CAP * PARTS) == lax.broadcasted_iota(jnp.int32, (chunk, experts), 1)
-        ).astype(BF16)
+        row = s + lax.broadcasted_iota(jnp.int32, (chunk, 1), 0)
+        expert = row // (CAP * PARTS)
+        owner = (expert == lax.broadcasted_iota(jnp.int32, (chunk, experts), 1)).astype(BF16)
         ranks = jnp.dot(owner, wide, preferred_element_type=F32)
-        row = s + lax.broadcasted_iota(jnp.int32, (chunk, width), 0)
-        col = lax.broadcasted_iota(jnp.int32, (chunk, width), 1)
-        hit = (ranks == (row // PARTS % CAP + 1).astype(F32)) & (row % PARTS == col // rows)
+        part = lax.broadcasted_iota(jnp.int32, (chunk, width), 1) // rows
+        hit = (ranks == (row // PARTS - CAP * expert + 1).astype(F32)) & (row % PARTS == part)
         place_ref[s : s + chunk, :] = hit.astype(BF16)
-        slot = s + lax.broadcasted_iota(jnp.int32, (experts, chunk), 1)
-        owner = (
-            slot // (CAP * PARTS) == lax.broadcasted_iota(jnp.int32, (experts, chunk), 0)
-        ).astype(BF16)
+        col = s + lax.broadcasted_iota(jnp.int32, (1, chunk), 1)
+        expert = col // (CAP * PARTS)
+        owner = (expert == lax.broadcasted_iota(jnp.int32, (experts, chunk), 0)).astype(BF16)
         ranks = jnp.dot(rank.astype(BF16), owner, preferred_element_type=F32)
         value = jnp.dot(gates.astype(BF16), owner, preferred_element_type=F32)
-        col = s + lax.broadcasted_iota(jnp.int32, (rows, chunk), 1)
-        value = jnp.where(ranks == (col // PARTS % CAP + 1).astype(F32), value, 0.0)
+        value = jnp.where(ranks == (col // PARTS - CAP * expert + 1).astype(F32), value, 0.0)
         for c in range(PARTS):
             mix_ref[c * rows : (c + 1) * rows, s : s + chunk] = jnp.where(
                 col % PARTS == c, value, 0.0
@@ -318,17 +314,10 @@
             rows_ref[g * group : (g + 1) * group, c * PART : (c + 1) * PART] = moved[
                 c * group : (c + 1) * group, :
             ]
-    for c in range(PARTS):
-        for n in range(0, 2 * EW, PART):
-            part = jnp.dot(
-                rows_ref[:, c * PART : (c + 1) * PART],
-                w1_ref[c * PART : (c + 1) * PART, n : n + PART],
-                preferred_element_type=F32,
-            )
-            if c == 0:
-                gated_ref[:, n : n + PART] = part
-            else:
-                gated_ref[:, n : n + PART] += part
+    for n in range(0, 2 * EW, PART):
+        gated_ref[:, n : n + PART] = jnp.dot(
+            rows_ref[...], w1_ref[:, n : n + PART], preferred_element_type=F32
+        )
     gate = gated_ref[:, :EW]
     active = (gate / (1.0 + jnp.exp(-gate)) * gated_ref[:, EW:]).astype(BF16)
     for c in range(PARTS):

time: 170 us -> 170 us (level)
  no operation moved by 1% of the time
where the time goes in v5:
time: 170 us
  blocking collectives  138 us (81%)
  Pallas kernels  25.4 us (15%)
  starting transfers between devices  4.13 us (2%)
    all_to_all x1, blocking collectives, shards(): lax.all_to_all(outgoing.reshape(exchanged), ('ctx', 'exp'), 0, 0, tiled=T...  48.1 us
    all_to_all x1, blocking collectives, shards(): lax.all_to_all(results.reshape(exchanged), ('ctx', 'exp'), 0, 0, tiled=True)  45.9 us
    all_to_all x1, blocking collectives, shards(): lax.all_to_all(jnp.broadcast_to(own[None], (blocks,) + own.shape), 'ctx',...  24.9 us
    all_to_all x1, blocking collectives, shards(): received = lax.all_to_all(projected, 'exp', 0, 0, tiled=True)  19.3 us
    pallas_call x1, Pallas kernels, shards(): pl.pallas_call(expert_kernel, out_shape=jax.ShapeDtypeStruct((slots * PAR...  9.15 us
    pallas_call x1, Pallas kernels, shards(): pl.pallas_call(functools.partial(attend_kernel, pairs=pairs, heads=heads)...  8.55 us
  transfers between devices with their start and end apart: 2, of which 0 were waited for; matrix products, arithmetic and copies ran while one was open for 0% of the time, Pallas kernels for 1%

profile of v5, /device:TPU:1, one launch (start us, length us, event | category | flops | bytes accessed | tf_op | source)
XLA Modules:
  0.0 169.7 jit_solution(575977128794577312)
XLA Ops:
  0.0 0.0 copy-start.1
  0.0 0.0 copy-start.2
  0.0 3.2 %shard_map.101 = (bf16[592,1792]{1,0:T(8,128)(2,1)}, bf16[128,1024]{1,0:T(8,128)(2,1)S(1)}) custom-call(s32[1]{0:T(128)} %bitcast.7.info_ref, bf16[512,4096]{1,0:T(8,128)(2,1)} %weight_ref.3, bf16[128,2,512]{2,1,0:T(2,128)(2,1)} %query_ref.1), custom_call_target="tpu_custom_call" | custom-call | bytes 5242880 | tf_op jit(solution)/shard_map/pallas_call | solution.py:405
  3.2 0.0 copy-start.3
  3.2 0.0 copy-start.4
  3.2 0.0 copy-start.5
  3.2 0.0 copy-start
  3.2 3.4 %collective-permute-start.1 = (bf16[592,1792]{1,0:T(8,128)(2,1)}, bf16[592,1792]{1,0:T(8,128)(2,1)}, u32[]{:S(2)}, u32[]{:S(2)}) collective-permute-start(bf16[592,1792]{1,0:T(8,128)(2,1)} %get-tuple-element.23), channel_id=1, source_target_pairs={{0,1},{1,0},{2,3},{3,2},{4,5},{5,4},{6,7},{7,6},{8,11},{9,10},{10,... | collective-permute-start | bytes 6365192 | tf_op jit(solution)/shard_map/ppermute | solution.py:421
  6.6 0.0 copy-done.1
  6.6 0.0 copy-done.2
  6.6 0.1 constant_dynamic-slice_fusion
  6.7 0.1 pad_maximum_fusion
  6.9 0.1 broadcast_in_dim.17
  7.0 24.9 %all_to_all.20 = bf16[8,128,512]{2,1,0:T(8,128)(2,1)S(1)} all-to-all(bf16[8,128,512]{2,1,0:T(8,128)(2,1)S(1)} %broadcast_in_dim.17), channel_id=1, replica_groups={{0,16,32,48,64,80,96,112},{8,24,40,56,72,88,104,120},{1,17,33,49,65,81,..., dimensions={0} | all-to-all | bytes 2097152 | tf_op jit(solution)/shard_map/all_to_all | solution.py:423
  31.9 0.7 collective-permute-start
  32.6 0.0 copy-done.3
  32.6 0.0 copy-done.4
  32.6 0.1 copy.11
  32.7 0.0 copy-done.5
  32.7 0.1 copy.12
  32.8 0.0 copy-done
  32.8 0.2 copy.13
  33.0 0.0 slice-start.3
  33.0 2.2 %shard_map.100 = (bf16[3072,256]{1,0:T(8,128)(2,1)S(1)}, bf16[256,3072]{1,0:T(8,128)(2,1)S(1)}) custom-call(s32[32,8]{1,0:T(8,128)S(1)} %bitcast.31, f32[32,8]{1,0:T(8,128)S(1)} %bitcast.32), custom_call_target="tpu_custom_call" | custom-call | flops 1000000000 | bytes 3145728 | tf_op jit(solution)/shard_map/pallas_call | solution.py:440
  35.2 0.1 compare_convert_fusion
  35.3 0.1 pad_add_fusion.info_ref
  35.3 0.0 collective-permute-done
  35.3 0.0 collective-permute-done.1.side_ref
  35.3 0.0 slice-start
  35.3 0.0 slice-start.1
  35.4 0.0 slice-start.4
  35.4 8.6 %shard_map.102 = bf16[8,32,2304]{2,1,0:T(8,128)(2,1)S(1)} custom-call(s32[17]{0:T(128)S(1)} %pad_add_fusion.info_ref, bf16[128,1024]{1,0:T(8,128)(2,1)S(1)} %get-tuple-element.22.q0_ref, bf16[128,512]{1,0:T(8,128)(2,1)S(1)} %bitcast.29, bf16[1024,512]{1,0:T(8,128)(2,1)S(1)} %bitcast.27, bf16[1024,512]{1,0:T(8,128)(2,1)S(1)} %bitcast.39, ...), custom_call_target="tpu_custom_call" | custom-call | flops 3000000000 | bytes 9437184 | tf_op jit(solution)/shard_map/pallas_call | solution.py:455
  43.9 19.3 %all_to_all.21.part_ref = bf16[8,32,2304]{2,1,0:T(8,128)(2,1)S(1)} all-to-all(bf16[8,32,2304]{2,1,0:T(8,128)(2,1)S(1)} %shard_map.102), channel_id=1, replica_groups=mesh['ctx'=16,'exp'=8] {'exp'}, dimensions={0} | all-to-all | bytes 2359296 | tf_op jit(solution)/shard_map/all_to_all | solution.py:485
  63.3 0.0 slice-start.2
  63.3 1.3 shard_map.103
  64.6 48.1 %all_to_all.22 = bf16[128,24,512]{2,1,0:T(8,128)(2,1)S(1)} all-to-all(bf16[128,24,512]{2,1,0:T(8,128)(2,1)S(1)} %bitcast.23), channel_id=1, replica_groups=mesh['ctx'=16,'exp'=8] {'ctx','exp'}, dimensions={0} | all-to-all | bytes 6291456 | tf_op jit(solution)/shard_map/all_to_all | solution.py:501
  112.6 0.0 slice-done.3
  112.7 0.0 slice-done
  112.7 0.0 slice-done.1
  112.7 0.0 slice-done.4
  112.7 0.0 slice-done.2
  112.7 9.2 %shard_map.104 = bf16[3072,512]{1,0:T(8,128)(2,1)S(1)} custom-call(bf16[3072,512]{1,0:T(8,128)(2,1)S(1)} %bitcast.24, bf16[4096,1536]{1,0:T(8,128)(2,1)S(1)} %bitcast.35, bf16[768,4096]{1,0:T(8,128)(2,1)S(1)} %bitcast.38), custom_call_target="tpu_custom_call" | custom-call | flops 8000000000 | bytes 6291456 | tf_op jit(solution)/shard_map/pallas_call | solution.py:504
  121.9 45.9 %all_to_all.23 = bf16[128,24,512]{2,1,0:T(8,128)(2,1)S(1)} all-to-all(bf16[128,24,512]{2,1,0:T(8,128)(2,1)S(1)} %bitcast.25), channel_id=1, replica_groups=mesh['ctx'=16,'exp'=8] {'ctx','exp'}, dimensions={0} | all-to-all | bytes 6291456 | tf_op jit(solution)/shard_map/all_to_all | solution.py:519
  167.7 1.0 shard_map.105
  168.7 1.0 copy.17
  (5 shorter events, 0.0 us)
Async XLA Ops:
  0.0 6.6 %copy-start.1 = (bf16[128,2,256]{2,1,0:T(2,128)(2,1)S(1)}, bf16[128,2,256]{2,1,0:T(2,128)(2,1)}, u32[]{:S(2)}) copy-start(bf16[128,2,256]{2,1,0:T(2,128)(2,1)} %param.13) | copy-start | bytes 393220
  0.0 6.6 %copy-start.2 = (bf16[128,2,256]{2,1,0:T(2,128)(2,1)S(1)}, bf16[128,2,256]{2,1,0:T(2,128)(2,1)}, u32[]{:S(2)}) copy-start(bf16[128,2,256]{2,1,0:T(2,128)(2,1)} %param.12) | copy-start | bytes 393220
  3.2 29.4 %copy-start.3 = (bf16[4096]{0:T(1024)(128)(2,1)S(1)}, bf16[4096]{0:T(1024)(128)(2,1)}, u32[]{:S(2)}) copy-start(bf16[4096]{0:T(1024)(128)(2,1)} %param.15) | copy-start | bytes 24580
  3.2 29.4 %copy-start.4 = (s32[16,2,8]{0,2,1:T(8,128)S(1)}, s32[16,2,8]{0,2,1:T(8,128)}, u32[]{:S(2)}) copy-start(s32[16,2,8]{0,2,1:T(8,128)} %param.16) | copy-start | bytes 3076
  3.2 29.5 %copy-start.5 = (f32[16,2,8]{0,2,1:T(8,128)S(1)}, f32[16,2,8]{0,2,1:T(8,128)}, u32[]{:S(2)}) copy-start(f32[16,2,8]{0,2,1:T(8,128)} %param.17) | copy-start | bytes 3076
  3.2 29.6 %copy-start = (bf16[16,2,4096]{2,1,0:T(2,128)(2,1)S(1)}, bf16[16,2,4096]{2,1,0:T(2,128)(2,1)}, u32[]{:S(2)}) copy-start(bf16[16,2,4096]{2,1,0:T(2,128)(2,1)} %param.10) | copy-start | bytes 786436
  3.2 32.1 %collective-permute-start.1 = (bf16[592,1792]{1,0:T(8,128)(2,1)}, bf16[592,1792]{1,0:T(8,128)(2,1)}, u32[]{:S(2)}, u32[]{:S(2)}) collective-permute-start(bf16[592,1792]{1,0:T(8,128)(2,1)} %get-tuple-element.23), channel_id=1, source_target_pairs={{0,1},{1,0},{2,3},{3,2},{4,5},{5,4},{6,7},{7,6},{8,11},{9,10},{10,... | collective-permute-start | bytes 6365192 | tf_op jit(solution)/shard_map/ppermute | solution.py:421
  31.9 3.5 %collective-permute-start = (bf16[8,128,512]{2,1,0:T(8,128)(2,1)S(1)}, bf16[8,128,512]{2,1,0:T(8,128)(2,1)S(1)}, u32[]{:S(2)}, u32[]{:S(2)}) collective-permute-start(bf16[8,128,512]{2,1,0:T(8,128)(2,1)S(1)} %all_to_all.20), channel_id=1, source_target_pairs={{0,8},{8,0},{16,24},{24,16},{32,40},{40,32},{48,56},{56,48},{64,72... | collective-permute-start | bytes 3145736 | tf_op jit(solution)/shard_map/ppermute | solution.py:431
  33.0 79.7 %slice-start.3 = ((s8[6291456]{0:T(1024)(128)(4,1)}), s8[4194304]{0:T(1024)(128)(4,1)S(1)}, s32[]{:S(2)}) async-start(s8[6291456]{0:T(1024)(128)(4,1)} %bitcast.36), calls=%async_computation.7 | async-start | bytes 8388608
  35.3 77.3 %slice-start = ((s8[12582912]{0:T(1024)(128)(4,1)}), s8[4194304]{0:T(1024)(128)(4,1)S(1)}, s32[]{:S(2)}) async-start(s8[12582912]{0:T(1024)(128)(4,1)} %bitcast.33), calls=%async_computation.4 | async-start | bytes 8388608
  35.3 77.3 %slice-start.1 = ((s8[12582912]{0:T(1024)(128)(4,1)}), s8[4194304]{0:T(1024)(128)(4,1)S(1)}, s32[]{:S(2)}) async-start(s8[12582912]{0:T(1024)(128)(4,1)} %bitcast.33), calls=%async_computation.5 | async-start | bytes 8388608
  35.4 77.3 %slice-start.4 = ((s8[6291456]{0:T(1024)(128)(4,1)}), s8[2097152]{0:T(1024)(128)(4,1)S(1)}, s32[]{:S(2)}) async-start(s8[6291456]{0:T(1024)(128)(4,1)} %bitcast.36), calls=%async_computation.8 | async-start | bytes 4194304
  63.3 49.4 %slice-start.2 = ((s8[12582912]{0:T(1024)(128)(4,1)}), s8[4194304]{0:T(1024)(128)(4,1)S(1)}, s32[]{:S(2)}) async-start(s8[12582912]{0:T(1024)(128)(4,1)} %bitcast.33), calls=%async_computation.6 | async-start | bytes 8388608
